TPU v7x, 512 devices: a whole 4x8x8 slice. The times are simulated.
512 devices in a mesh: rows: 32 (over x, z), feat: 16 (over y, core).
Axes of the slice: x: 4, y: 8, z: 8, core: 2. Of those that a mesh axis runs over, the one named last changes fastest.
Arguments:
- block_values: bfloat16 [32, 16, 12, 128, 128], P('rows', 'feat'), may hold values from -6 to 6
- block_rows: int32 [32, 16, 12], P('rows', 'feat'), may hold values from 0 to 3, as said below
- block_cols: int32 [32, 16, 12], P('rows', 'feat'), may hold values from 0 to 3, as said below
- test_matrix: bfloat16 [8192, 256], P('feat'), may hold values from -18 to 18
Outputs:
- doc_basis: float32 [16384, 256], P(('rows', 'feat'))
Inputs may be any that keep to these rules, and one draw needn't show every extreme that they name: Within one tile the 12 pairs (block_rows, block_cols) are distinct, and every block row and every block column of the tile occurs among them. `block_cols`: see block_rows: paired entry by entry with it.
All inputs are finite; a program needn't handle non-finite values.
Results may differ from a plain program's by a relative error of at most 0.0034.
Values may be sent and summed in bfloat16 or wider, within the bound.
No kernel may reach another device: no remote copies, remote signals or barrier semaphores. Data moves between devices by JAX's collectives and lax.ppermute only.
A program may use at most 64 MiB of HBM per device.

v0:
```python
import jax
import jax.numpy as jnp
from jax import lax
from jax.sharding import PartitionSpec as P


def tile_rows(values, rows_idx, cols_idx, basis):
    count = basis.shape[0] // values.shape[-1]
    width = values.shape[-1]
    pieces = basis.reshape(count, width, basis.shape[1])[cols_idx]
    prod = jnp.einsum("nij,njr->nir", values, pieces, preferred_element_type=jnp.float32)
    onehot = (rows_idx[None, :] == jnp.arange(count)[:, None]).astype(jnp.float32)
    summed = jnp.einsum("kn,nir->kir", onehot, prod, precision=lax.Precision.HIGHEST)
    return summed.reshape(count * width, basis.shape[1])


def tile_cols(values, rows_idx, cols_idx, basis):
    count = basis.shape[0] // values.shape[-1]
    width = values.shape[-1]
    pieces = basis.reshape(count, width, basis.shape[1])[rows_idx]
    prod = jnp.einsum("nij,nir->njr", values, pieces, preferred_element_type=jnp.float32)
    onehot = (cols_idx[None, :] == jnp.arange(count)[:, None]).astype(jnp.float32)
    summed = jnp.einsum("kn,nir->kir", onehot, prod, precision=lax.Precision.HIGHEST)
    return summed.reshape(count * width, basis.shape[1])


def gram_of(matrix):
    return jnp.einsum("dr,ds->rs", matrix, matrix, precision=lax.Precision.HIGHEST)


def whiten_with(matrix, gram):
    lower = jnp.linalg.cholesky(gram)
    identity = jnp.eye(gram.shape[0], dtype=gram.dtype)
    inverse = lax.linalg.triangular_solve(lower, identity, left_side=True, lower=True)
    return jnp.dot(matrix, inverse.T, precision=lax.Precision.HIGHEST)


def per_device(block_values, block_rows, block_cols, test_matrix):
    values = block_values[0, 0]
    rows_idx = block_rows[0, 0]
    cols_idx = block_cols[0, 0]
    local_docs = values.shape[-1] * (test_matrix.shape[0] // values.shape[-1])
    total_docs = local_docs * lax.axis_size("rows")
    scale = jnp.sqrt(jnp.float32(total_docs))

    def doc_total(basis):
        return lax.psum(tile_rows(values, rows_idx, cols_idx, basis), "feat")

    def doc_whiten(sketch):
        return whiten_with(sketch, lax.psum(gram_of(sketch), "rows"))

    basis = doc_whiten(doc_total(test_matrix)).astype(jnp.bfloat16)
    cosketch = lax.psum(tile_cols(values, rows_idx, cols_idx, basis), "rows")
    cobasis = cosketch.astype(jnp.bfloat16)
    final = doc_whiten(doc_total(cobasis)) * scale
    share = local_docs // lax.axis_size("feat")
    return lax.dynamic_slice_in_dim(final, lax.axis_index("feat") * share, share, 0)


def solution(mesh):
    placed = (
        P("rows", "feat", None, None, None),
        P("rows", "feat", None),
        P("rows", "feat", None),
        P("feat", None),
    )
    return jax.shard_map(
        per_device, mesh=mesh, in_specs=placed, out_specs=P(("rows", "feat"), None), check_vma=False
    )
```

profile of v0, /device:TPU:1, one launch (start us, length us, event | category | flops | bytes accessed | tf_op | source)
XLA Modules:
  0.0 851.0 jit_solution(8236123980438517504)
XLA Ops:
  6.5 0.7 fusion.44
  7.3 1.5 gather_fusion
  8.8 1.6 fusion.10
  10.4 2.2 copy.16
  12.6 0.8 fusion.4
  13.5 0.9 copy.9
  14.4 120.4 %all-reduce.7.cloned.1.call-done = f32[512,256]{1,0:T(8,128)} async-done(((f32[512,256]{1,0:T(8,128)}), f32[512,256]{1,0:T(8,128)}) %all-reduce.7.cloned.1.call-update) | async-done | bytes 524304 | tf_op jit(solution)/shard_map/psum | solution.py:47
  134.9 2.9 fusion.50
  138.4 152.2 %all-reduce.9.cloned.1.call-done = f32[256,256]{0,1:T(8,128)} async-done(((f32[256,256]{0,1:T(8,128)}), f32[256,256]{0,1:T(8,128)}) %all-reduce.9.cloned.1.call-update) | async-done | bytes 262160 | tf_op jit(solution)/shard_map/psum | solution.py:50
  290.6 1.1 copy.11
  291.7 1.0 fusion.20
  292.7 11.7 %cholesky.130 = f32[128,128]{1,0:T(8,128)S(1)} custom-call(f32[128,128]{1,0:T(8,128)S(1)} %cholesky.194), custom_call_target="Cholesky" | custom-call | tf_op jit(solution)/shard_map/jit(cholesky)/cholesky | solution.py:32
  304.5 9.8 %custom-call.13 = f32[1,128,128]{1,2,0:T(8,128)S(1)} custom-call(f32[1,128,128]{2,1,0:T(8,128)S(1)} %get-tuple-element.50), custom_call_target="InvertDiagBlocksLowerTriangular" | custom-call | tf_op jit(solution)/shard_map/jit(cholesky)/cholesky | solution.py:32
  314.8 11.7 %cholesky.147 = f32[128,128]{1,0:T(8,128)S(1)} custom-call(f32[128,128]{1,0:T(8,128)S(1)} %convolution_subtract_fusion.3), custom_call_target="Cholesky" | custom-call | tf_op jit(solution)/shard_map/jit(cholesky)/cholesky | solution.py:32
  326.6 0.7 compare_reduce_fusion.2
  328.7 4.3 while.4
  328.9 0.7 fusion.71
  329.5 1.3 bitcast_dynamic-update-slice_fusion.4
  330.9 0.7 fusion.71
  331.6 1.3 bitcast_dynamic-update-slice_fusion.4
  332.9 19.7 %custom-call.14 = f32[2,128,128]{1,2,0:T(8,128)S(1)} custom-call(f32[2,128,128]{2,1,0:T(8,128)S(1)} %get-tuple-element.21), custom_call_target="InvertDiagBlocksLowerTriangular" | custom-call | tf_op jit(solution)/shard_map/triangular_solve/custom-call.0 | solution.py:34
  353.5 0.6 convolution_convert_fusion
  354.8 1.6 fusion.8
  356.3 2.2 copy.18
  358.6 0.8 fusion.2
  359.5 117.2 %all-reduce.14 = bf16[512,256]{1,0:T(8,128)(2,1)S(1)} all-reduce(f32[512,256]{1,0:T(8,128)S(1)} %bitcast.115), channel_id=1, replica_groups=mesh['rows'=32,'feat'=16] {'rows'}, use_global_device_ids=true, to_apply=%region_6.9 | all-reduce | flops 131072 | bytes 786432 | tf_op jit(solution)/shard_map/psum | solution.py:53
  477.3 1.6 fusion.6
  478.9 2.2 copy.19
  481.1 0.8 fusion
  481.9 0.9 copy.13
  483.1 141.0 %all-reduce.11.cloned.1.call-done = f32[512,256]{1,0:T(8,128)} async-done(((f32[512,256]{1,0:T(8,128)}), f32[512,256]{1,0:T(8,128)}) %all-reduce.11.cloned.1.call-update) | async-done | bytes 524304 | tf_op jit(solution)/shard_map/psum | solution.py:47
  624.1 2.9 fusion.51
  627.1 152.3 %all-reduce.13.cloned.1.call-done = f32[256,256]{0,1:T(8,128)} async-done(((f32[256,256]{0,1:T(8,128)}), f32[256,256]{0,1:T(8,128)}) %all-reduce.13.cloned.1.call-update) | async-done | bytes 262160 | tf_op jit(solution)/shard_map/psum | solution.py:50
  779.4 1.1 copy.15
  780.5 1.0 fusion.19
  781.5 11.7 %cholesky.164 = f32[128,128]{1,0:T(8,128)S(1)} custom-call(f32[128,128]{1,0:T(8,128)S(1)} %cholesky.197), custom_call_target="Cholesky" | custom-call | tf_op jit(solution)/shard_map/jit(cholesky)/cholesky | solution.py:32
  793.3 9.8 %custom-call.15 = f32[1,128,128]{1,2,0:T(8,128)S(1)} custom-call(f32[1,128,128]{2,1,0:T(8,128)S(1)} %get-tuple-element.46), custom_call_target="InvertDiagBlocksLowerTriangular" | custom-call | tf_op jit(solution)/shard_map/jit(cholesky)/cholesky | solution.py:32
  803.6 11.7 %cholesky.181 = f32[128,128]{1,0:T(8,128)S(1)} custom-call(f32[128,128]{1,0:T(8,128)S(1)} %convolution_subtract_fusion.2), custom_call_target="Cholesky" | custom-call | tf_op jit(solution)/shard_map/jit(cholesky)/cholesky | solution.py:32
  815.3 0.6 compare_reduce_fusion
  816.0 0.7 compare_reduce_fusion.1
  818.0 4.3 while.5
  818.3 0.7 fusion.72
  818.9 1.3 bitcast_dynamic-update-slice_fusion.5
  820.3 0.7 fusion.72
  821.0 1.3 bitcast_dynamic-update-slice_fusion.5
  822.3 19.7 %custom-call.16 = f32[2,128,128]{1,2,0:T(8,128)S(1)} custom-call(f32[2,128,128]{2,1,0:T(8,128)S(1)} %get-tuple-element.22), custom_call_target="InvertDiagBlocksLowerTriangular" | custom-call | tf_op jit(solution)/shard_map/triangular_solve/custom-call.0 | solution.py:34
  842.9 0.6 fusion.15
  843.6 0.6 dynamic-slice_multiply_fusion
  (53 shorter events, 5.4 us)
Async XLA Ops:
  6.5 2.3 copy-start
  6.5 128.3 %all-reduce.7.cloned.1.call-start = ((), (), s32[]{:S(2)}) async-start(), calls=%async_computation | async-start | bytes 1048576 | tf_op jit(solution)/shard_map/psum | solution.py:47
  10.4 2.2 copy-start.3
  14.4 276.2 %all-reduce.9.cloned.1.call-start = ((), (), s32[]{:S(2)}) async-start(), calls=%async_computation.1 | async-start | bytes 524288 | tf_op jit(solution)/shard_map/psum | solution.py:50
  137.8 486.4 %all-reduce.11.cloned.1.call-start = ((), (), s32[]{:S(2)}) async-start(), calls=%async_computation.2 | async-start | bytes 1048576 | tf_op jit(solution)/shard_map/psum | solution.py:47
  292.7 60.8 %copy-start.2 = (f32[512,256]{1,0:T(8,128)S(1)}, f32[512,256]{1,0:T(8,128)}, u32[]{:S(2)}) copy-start(f32[512,256]{1,0:T(8,128)} %all-reduce.7.cloned.1.call-done) | copy-start | bytes 1572868
  356.3 2.2 copy-start.4
  482.8 296.6 %all-reduce.13.cloned.1.call-start = ((), (), s32[]{:S(2)}) async-start(), calls=%async_computation.3 | async-start | bytes 524288 | tf_op jit(solution)/shard_map/psum | solution.py:50
  781.5 61.5 %copy-start.1 = (f32[512,256]{1,0:T(8,128)S(1)}, f32[512,256]{1,0:T(8,128)}, u32[]{:S(2)}) copy-start(f32[512,256]{1,0:T(8,128)} %all-reduce.11.cloned.1.call-done) | copy-start | bytes 1572868
Sparse Core Ops, SparseCore 0:
  14.5 120.2 all-reduce.6
  138.7 151.8 all-reduce.8
  483.0 141.1 all-reduce.10
  627.4 151.9 all-reduce.12
where the time goes:
time: 858 us; the launch traced here: 851 us
  waiting for transfers between devices  566 us (66%)
  blocking collectives  117 us (14%)
  other arithmetic  111 us (13%)
  local copies, waits for them, and re-layouts  21.7 us (3%)
  matrix products  16.9 us (2%)
  between operations  16.3 us (2%)
    psum x2, waiting for transfers between devices, doc_whiten(): return whiten_with(sketch, lax.psum(gram_of(sketch), 'rows'))  305 us
    psum x2, waiting for transfers between devices, doc_total(): return lax.psum(tile_rows(values, rows_idx, cols_idx, basis), 'feat')  261 us
    psum x1, blocking collectives, per_device(): cosketch = lax.psum(tile_cols(values, rows_idx, cols_idx, basis), 'rows')  117 us
    another operation x13, other arithmetic, whiten_with(): lower = jnp.linalg.cholesky(gram)  68.7 us
    another operation x5, other arithmetic, whiten_with(): lax.linalg.triangular_solve(lower, identity, left_side=True, lower=True)  39.4 us
  transfers between devices with their start and end apart: 4, of which 4 were waited for; matrix products, arithmetic and copies ran while one was open for 0% of the time, Pallas kernels for 0%

commit v1 on v0

v1 whole, which is shorter than its diff:
```python
import jax
import jax.numpy as jnp
from jax import lax
from jax.experimental import pallas as pl
from jax.experimental.pallas import tpu as pltpu
from jax.sharding import PartitionSpec as P

HIGHEST = lax.Precision.HIGHEST
VMEM = pl.BlockSpec(memory_space=pltpu.VMEM)
SMEM = pl.BlockSpec(memory_space=pltpu.SMEM)


def dot(a, b, precision=None):
    return jnp.dot(a, b, preferred_element_type=jnp.float32, precision=precision)


def dot_t(a, b, precision=None):
    dims = (((0,), (0,)), ((), ()))
    return lax.dot_general(a, b, dims, preferred_element_type=jnp.float32, precision=precision)


def first_kernel(rows_ref, cols_ref, values_ref, test_ref, tile_ref, part_ref):
    count, width = values_ref.shape[0], values_ref.shape[1]
    tile_ref[...] = jnp.zeros_like(tile_ref)
    for n in range(count):
        row = pl.multiple_of(rows_ref[n] * width, width)
        col = pl.multiple_of(cols_ref[n] * width, width)
        tile_ref[pl.ds(row, width), pl.ds(col, width)] = values_ref[n]
    part_ref[...] = dot(tile_ref[...], test_ref[...]).reshape(part_ref.shape)


def second_kernel(tile_ref, sketch_ref, out_ref):
    sketch = sketch_ref[...]
    tile = tile_ref[...]
    groups = out_ref.shape[0]
    rank = sketch.shape[1]
    high = sketch.astype(jnp.bfloat16)
    rest = sketch - high.astype(jnp.float32)
    mid = rest.astype(jnp.bfloat16)
    low = (rest - mid.astype(jnp.float32)).astype(jnp.bfloat16)
    co = dot_t(tile, high) + (dot_t(tile, mid) + dot_t(tile, low))
    split = tile.shape[1] // groups
    out_ref[:, :split, :] = co.reshape(groups, split, rank)
    gram = dot_t(sketch, sketch, HIGHEST)
    out_ref[:, split:, :] = gram.reshape(groups, rank // groups, rank)


def inverse_factor(gram):
    lower = jnp.linalg.cholesky(gram)
    identity = jnp.eye(gram.shape[0], dtype=gram.dtype)
    return lax.linalg.triangular_solve(lower, identity, left_side=True, lower=True)


def to_each(x, axis):
    return lax.all_to_all(x, axis, 0, 0, tiled=True)


def from_each(x, axis):
    size = lax.axis_size(axis)
    return to_each(jnp.broadcast_to(x[None], (size,) + x.shape), axis)


def per_device(block_values, block_rows, block_cols, test_matrix):
    values = block_values[0, 0]
    side, rank = test_matrix.shape
    n_rows, n_feat = lax.axis_size("rows"), lax.axis_size("feat")
    scale = jnp.sqrt(jnp.float32(side * n_rows))
    share = side // n_feat
    split = side // n_rows

    tile, part = pl.pallas_call(
        first_kernel,
        in_specs=[SMEM, SMEM, VMEM, VMEM],
        out_specs=[VMEM, VMEM],
        out_shape=[
            jax.ShapeDtypeStruct((side, side), jnp.bfloat16),
            jax.ShapeDtypeStruct((n_feat, share, rank), jnp.float32),
        ],
    )(block_rows[0, 0], block_cols[0, 0], values, test_matrix)
    sketch = lax.all_gather(jnp.sum(to_each(part, "feat"), axis=0), "feat", axis=0, tiled=True)

    both = pl.pallas_call(
        second_kernel,
        in_specs=[VMEM, VMEM],
        out_specs=VMEM,
        out_shape=jax.ShapeDtypeStruct((n_rows, split + rank // n_rows, rank), jnp.float32),
    )(tile, sketch)
    both = from_each(jnp.sum(to_each(both, "rows"), axis=0), "rows")
    cosketch = both[:, :split].reshape(side, rank)
    inverse = inverse_factor(both[:, split:].reshape(rank, rank))
    cobasis = jnp.dot(cosketch, inverse.T, precision=HIGHEST).astype(jnp.bfloat16)

    part = dot(tile, cobasis).reshape(n_feat, share, rank)
    resketch = jnp.sum(to_each(part, "feat"), axis=0)
    gram = dot_t(resketch, resketch, HIGHEST).reshape(n_rows, rank // n_rows, rank)
    gram = jnp.sum(to_each(gram, "rows"), axis=0)
    gram = jnp.sum(lax.all_gather(gram, "feat", axis=0), axis=0)
    gram = from_each(gram, "rows").reshape(rank, rank)
    return jnp.dot(resketch, inverse_factor(gram).T, precision=HIGHEST) * scale


def solution(mesh):
    placed = (
        P("rows", "feat", None, None, None),
        P("rows", "feat", None),
        P("rows", "feat", None),
        P("feat", None),
    )
    return jax.shard_map(
        per_device, mesh=mesh, in_specs=placed, out_specs=P(("rows", "feat"), None), check_vma=False
    )
```

time: 858 us -> 310 us (0.36)
  waiting for transfers between devices: 566 us -> 37 us
  starting transfers between devices: 0.86 us -> 18.3 us
  between operations: 16.3 us -> 2.8 us
  matrix products: 16.9 us -> 4.92 us
  local copies, waits for them, and re-layouts: 21.7 us -> 9.97 us
    psum x4 -> x0, waiting for transfers between devices: 566 us -> none  [the longest x2 305 us: doc_whiten(): return whiten_with(sketch, lax.psum(gram_of(sketch), 'rows'))]
    psum x1 -> x0, blocking collectives: 117 us -> none  [per_device(): cosketch = lax.psum(tile_cols(values, rows_idx, cols_idx, basis), 'rows')]
    all_to_all x0 -> x4, blocking collectives: none -> 87.6 us  [to_each(): return lax.all_to_all(x, axis, 0, 0, tiled=True)]
    all_to_all x0 -> x2, waiting for transfers between devices: none -> 37 us  [to_each(): return lax.all_to_all(x, axis, 0, 0, tiled=True)]
    all_gather x0 -> x2, blocking collectives: none -> 32.7 us  [the longest x1 17.3 us: per_device(): lax.all_gather(jnp.sum(to_each(part, 'feat'), axis=0), 'feat', axis=0, ti...]
    all_to_all x0 -> x2, starting transfers between devices: none -> 18.3 us  [to_each(): return lax.all_to_all(x, axis, 0, 0, tiled=True)]
    dot_general x10 -> x4, matrix products: 14.2 us -> 2.22 us  [the longest x1 0.96 us: per_device(): return jnp.dot(resketch, inverse_factor(gram).T, precision=HIGHEST) * scale]
  transfers between devices with their start and end apart: 4 -> 2, of which waited for: 4 -> 2; matrix products, arithmetic and copies ran while one was open for 0% -> 0% of each run, Pallas kernels for 0% -> 0%
where the time goes in v1:
time: 310 us; the launch traced here: 308 us
  blocking collectives  120 us (39%)
  other arithmetic  109 us (35%)
  waiting for transfers between devices  37 us (12%)
  starting transfers between devices  18.3 us (6%)
  local copies, waits for them, and re-layouts  9.97 us (3%)
  Pallas kernels  5.4 us (2%)
  matrix products  4.92 us (2%)
    all_to_all x4, blocking collectives, to_each(): return lax.all_to_all(x, axis, 0, 0, tiled=True)  87.6 us
    another operation x13, other arithmetic, inverse_factor(): lower = jnp.linalg.cholesky(gram)  68.7 us
    another operation x5, other arithmetic, inverse_factor(): lax.linalg.triangular_solve(lower, identity, left_side=True, lower=True)  39.9 us
    all_to_all x2, waiting for transfers between devices, to_each(): return lax.all_to_all(x, axis, 0, 0, tiled=True)  37 us
    all_to_all x2, starting transfers between devices, to_each(): return lax.all_to_all(x, axis, 0, 0, tiled=True)  18.3 us
    all_gather x1, blocking collectives, per_device(): lax.all_gather(jnp.sum(to_each(part, 'feat'), axis=0), 'feat', axis=0, ti...  17.3 us
    all_gather x1, blocking collectives, per_device(): gram = jnp.sum(lax.all_gather(gram, 'feat', axis=0), axis=0)  15.4 us
    another operation x15, local copies, waits for them, and re-layouts, inverse_factor(): lax.linalg.triangular_solve(lower, identity, left_side=True, lower=True)  8.13 us
  transfers between devices with their start and end apart: 2, of which 2 were waited for; matrix products, arithmetic and copies ran while one was open for 0% of the time, Pallas kernels for 0%

profile of v1, /device:TPU:1, one launch (start us, length us, event | category | flops | bytes accessed | tf_op | source)
XLA Modules:
  0.0 307.6 jit_solution(15346869035138090073)
XLA Ops:
  0.0 2.2 shard_map.46
  2.2 10.2 %all-to-all-start = ((f32[16,32,256]{2,1,0:T(8,128)}), f32[16,32,256]{2,1,0:T(8,128)S(1)}, u32[]{:S(2)}, u32[]{:S(2)}) async-start(f32[16,32,256]{2,1,0:T(8,128)} %get-tuple-element.10), calls=%async_computation | async-start | bytes 1048576 | tf_op jit(solution)/shard_map/all_to_all | solution.py:55
  12.5 17.3 %all-to-all-done = f32[16,32,256]{2,1,0:T(8,128)S(1)} async-done(((f32[16,32,256]{2,1,0:T(8,128)}), f32[16,32,256]{2,1,0:T(8,128)S(1)}, u32[]{:S(2)}, u32[]{:S(2)}) %all-to-all-start) | async-done | bytes 524320 | tf_op jit(solution)/shard_map/all_to_all | solution.py:55
  29.9 17.3 %all_gather.9.sketch_ref = f32[512,256]{1,0:T(8,128)} all-gather(f32[32,256]{1,0:T(8,128)S(1)} %reduce_sum.45), channel_id=1, replica_groups=mesh['rows'=32,'feat'=16] {'feat'}, dimensions={0}, use_global_device_ids=true | all-gather | bytes 557056 | tf_op jit(solution)/shard_map/all_gather | solution.py:80
  47.2 3.2 %shard_map.47 = f32[32,24,256]{2,1,0:T(8,128)} custom-call(bf16[512,512]{1,0:T(8,128)(2,1)} %get-tuple-element.9.tile_ref, f32[512,256]{1,0:T(8,128)} %all_gather.9.sketch_ref), custom_call_target="tpu_custom_call" | custom-call | tf_op jit(solution)/shard_map/pallas_call | solution.py:82
  50.3 31.1 %all_to_all.30 = f32[32,24,256]{2,1,0:T(8,128)S(1)} all-to-all(f32[32,24,256]{2,1,0:T(8,128)} %shard_map.47), channel_id=1, replica_groups=mesh['rows'=32,'feat'=16] {'rows'}, dimensions={0} | all-to-all | bytes 1572864 | tf_op jit(solution)/shard_map/all_to_all | solution.py:55
  81.4 0.9 broadcast_in_dim.4
  82.4 8.1 %all-to-all-start.2 = ((f32[32,24,256]{2,1,0:T(8,128)}), f32[32,24,256]{2,1,0:T(8,128)S(1)}, u32[]{:S(2)}, u32[]{:S(2)}) async-start(f32[32,24,256]{2,1,0:T(8,128)} %broadcast_in_dim.4), calls=%async_computation.2 | async-start | bytes 1572864 | tf_op jit(solution)/shard_map/all_to_all | solution.py:55
  90.5 19.6 %all-to-all-done.2 = f32[32,24,256]{2,1,0:T(8,128)S(1)} async-done(((f32[32,24,256]{2,1,0:T(8,128)}), f32[32,24,256]{2,1,0:T(8,128)S(1)}, u32[]{:S(2)}, u32[]{:S(2)}) %all-to-all-start.2) | async-done | bytes 786464 | tf_op jit(solution)/shard_map/all_to_all | solution.py:55
  110.3 11.7 %cholesky.130 = f32[128,128]{1,0:T(8,128)S(1)} custom-call(f32[128,128]{1,0:T(8,128)S(1)} %cholesky.194), custom_call_target="Cholesky" | custom-call | tf_op jit(solution)/shard_map/jit(cholesky)/cholesky | solution.py:49
  122.1 9.8 %custom-call.13 = f32[1,128,128]{1,2,0:T(8,128)S(1)} custom-call(f32[1,128,128]{2,1,0:T(8,128)S(1)} %get-tuple-element.54), custom_call_target="InvertDiagBlocksLowerTriangular" | custom-call | tf_op jit(solution)/shard_map/jit(cholesky)/cholesky | solution.py:49
  132.1 0.3 convolution_subtract_fusion.3
  132.4 11.7 %cholesky.147 = f32[128,128]{1,0:T(8,128)S(1)} custom-call(f32[128,128]{1,0:T(8,128)S(1)} %convolution_subtract_fusion.3), custom_call_target="Cholesky" | custom-call | tf_op jit(solution)/shard_map/jit(cholesky)/cholesky | solution.py:49
  144.2 0.7 compare_reduce_fusion.2
  146.3 4.1 %while.4 = (s32[]{:T(128)}, f32[256,256]{1,0:T(8,128)S(1)}, s32[2,2]{1,0:T(2,128)S(1)}, f32[2,128,128]{2,1,0:T(8,128)S(1)}, s32[]{:T(128)}) while((s32[]{:T(128)}, f32[256,256]{1,0:T(8,128)S(1)}, s32[2,2]{1,0:T(2,128)S(1)}, f32[2,128,128]{2,1,0:T(8,128)S(1)}, s32[]{:T(128)}) %tuple.43), condition=%wide.while_cond, body=%wide.while_body.sunk | while | flops 2 | bytes 131181 | solution.py:51
  146.3 0.7 fusion.45
  147.0 1.3 bitcast_dynamic-update-slice_fusion.4
  148.3 0.7 fusion.45
  149.0 1.3 bitcast_dynamic-update-slice_fusion.4
  150.3 19.9 %custom-call.14 = f32[2,128,128]{1,2,0:T(8,128)S(1)} custom-call(f32[2,128,128]{2,1,0:T(8,128)S(1)} %get-tuple-element.25), custom_call_target="InvertDiagBlocksLowerTriangular" | custom-call | tf_op jit(solution)/shard_map/triangular_solve/custom-call.0 | solution.py:51
  170.2 0.3 fusion.13
  170.6 0.3 convolution_subtract_fusion.1
  170.8 0.3 fusion.20
  171.2 0.6 convolution_convert_fusion
  171.8 0.4 copy-done
  172.3 0.3 fusion.30
  172.6 26.5 %all_to_all.31 = f32[16,32,256]{2,1,0:T(8,128)S(1)} all-to-all(f32[16,32,256]{2,1,0:T(8,128)S(1)} %bitcast.88), channel_id=1, replica_groups=mesh['rows'=32,'feat'=16] {'feat'}, dimensions={0} | all-to-all | bytes 1048576 | tf_op jit(solution)/shard_map/all_to_all | solution.py:55
  199.2 0.3 fusion.9
  199.6 15.5 %all_to_all.32 = f32[32,8,256]{2,1,0:T(8,128)S(1)} all-to-all(f32[32,8,256]{2,1,0:T(8,128)S(1)} %fusion.9), channel_id=1, replica_groups=mesh['rows'=32,'feat'=16] {'rows'}, dimensions={0} | all-to-all | bytes 524288 | tf_op jit(solution)/shard_map/all_to_all | solution.py:55
  215.2 15.4 %all-gather = f32[128,256]{1,0:T(8,128)S(1)} all-gather(f32[8,256]{1,0:T(8,128)S(1)} %reduce_sum.48), channel_id=2, replica_groups=mesh['rows'=32,'feat'=16] {'feat'}, dimensions={0}, use_global_device_ids=true | all-gather | bytes 139264 | tf_op jit(solution)/shard_map/all_gather | solution.py:97
  230.6 14.4 %all_to_all.33 = f32[32,8,256]{2,1,0:T(8,128)S(1)} all-to-all(f32[32,8,256]{2,1,0:T(8,128)S(1)} %broadcast_in_dim.6), channel_id=1, replica_groups=mesh['rows'=32,'feat'=16] {'rows'}, dimensions={0} | all-to-all | bytes 524288 | tf_op jit(solution)/shard_map/all_to_all | solution.py:55
  245.3 11.7 %cholesky.164 = f32[128,128]{1,0:T(8,128)S(1)} custom-call(f32[128,128]{1,0:T(8,128)S(1)} %cholesky.197), custom_call_target="Cholesky" | custom-call | tf_op jit(solution)/shard_map/jit(cholesky)/cholesky | solution.py:49
  257.0 9.8 %custom-call.15 = f32[1,128,128]{1,2,0:T(8,128)S(1)} custom-call(f32[1,128,128]{2,1,0:T(8,128)S(1)} %get-tuple-element.50), custom_call_target="InvertDiagBlocksLowerTriangular" | custom-call | tf_op jit(solution)/shard_map/jit(cholesky)/cholesky | solution.py:49
  266.8 0.2 constant_dynamic-update-slice_fusion.1
  267.1 0.3 convolution_subtract_fusion.2
  267.3 11.7 %cholesky.181 = f32[128,128]{1,0:T(8,128)S(1)} custom-call(f32[128,128]{1,0:T(8,128)S(1)} %convolution_subtract_fusion.2), custom_call_target="Cholesky" | custom-call | tf_op jit(solution)/shard_map/jit(cholesky)/cholesky | solution.py:49
  279.1 0.6 compare_reduce_fusion
  279.7 0.7 compare_reduce_fusion.1
  281.7 4.1 %while.5 = (s32[]{:T(128)}, f32[256,256]{1,0:T(8,128)S(1)}, s32[2,2]{1,0:T(2,128)S(1)}, f32[2,128,128]{2,1,0:T(8,128)S(1)}, s32[]{:T(128)}) while((s32[]{:T(128)}, f32[256,256]{1,0:T(8,128)S(1)}, s32[2,2]{1,0:T(2,128)S(1)}, f32[2,128,128]{2,1,0:T(8,128)S(1)}, s32[]{:T(128)}) %tuple.49), condition=%wide.while_cond.clone, body=%wide.while_body.clone.sunk | while | flops 2 | bytes 131181 | solution.py:51
  281.8 0.7 fusion.46
  282.4 1.3 bitcast_dynamic-update-slice_fusion.5
  283.8 0.7 fusion.46
  284.5 1.3 bitcast_dynamic-update-slice_fusion.5
  285.8 19.9 %custom-call.16 = f32[2,128,128]{1,2,0:T(8,128)S(1)} custom-call(f32[2,128,128]{2,1,0:T(8,128)S(1)} %get-tuple-element.26), custom_call_target="InvertDiagBlocksLowerTriangular" | custom-call | tf_op jit(solution)/shard_map/triangular_solve/custom-call.0 | solution.py:51
  305.8 0.3 fusion.11
  306.1 0.3 convolution_subtract_fusion
  306.3 0.3 fusion.16
  306.7 1.0 convolution_multiply_fusion
  (34 shorter events, 1.3 us)
Async XLA Ops:
  2.2 27.6 %all-to-all-start = ((f32[16,32,256]{2,1,0:T(8,128)}), f32[16,32,256]{2,1,0:T(8,128)S(1)}, u32[]{:S(2)}, u32[]{:S(2)}) async-start(f32[16,32,256]{2,1,0:T(8,128)} %get-tuple-element.10), calls=%async_computation | async-start | bytes 1048576 | tf_op jit(solution)/shard_map/all_to_all | solution.py:55
  82.4 27.7 %all-to-all-start.2 = ((f32[32,24,256]{2,1,0:T(8,128)}), f32[32,24,256]{2,1,0:T(8,128)S(1)}, u32[]{:S(2)}, u32[]{:S(2)}) async-start(f32[32,24,256]{2,1,0:T(8,128)} %broadcast_in_dim.4), calls=%async_computation.2 | async-start | bytes 1572864 | tf_op jit(solution)/shard_map/all_to_all | solution.py:55
  171.2 1.0 copy-start

commit v2 on v1

v2 whole, which is shorter than its diff:
```python
import jax
import jax.numpy as jnp
from jax import lax
from jax.experimental import pallas as pl
from jax.experimental.pallas import tpu as pltpu
from jax.sharding import PartitionSpec as P

HIGHEST = lax.Precision.HIGHEST
VMEM = pl.BlockSpec(memory_space=pltpu.VMEM)
SMEM = pl.BlockSpec(memory_space=pltpu.SMEM)
SUB = 8


def dot(a, b, precision=None, contract=(1, 0)):
    dims = (((contract[0],), (contract[1],)), ((), ()))
    return lax.dot_general(a, b, dims, preferred_element_type=jnp.float32, precision=precision)


def terms(x):
    high = x.astype(jnp.bfloat16)
    rest = x - high.astype(jnp.float32)
    mid = rest.astype(jnp.bfloat16)
    return high, mid, (rest - mid.astype(jnp.float32)).astype(jnp.bfloat16)


def dot_terms(tile, x, contract=(1, 0)):
    high, mid, low = terms(x)
    small = dot(tile, mid, contract=contract) + dot(tile, low, contract=contract)
    return dot(tile, high, contract=contract) + small


def block_inverse(block):
    n = block.shape[0]
    shape = (SUB, n)
    parts = [block[i : i + SUB] for i in range(0, n, SUB)]
    lane = lax.broadcasted_iota(jnp.int32, shape, 1)
    sub = lax.broadcasted_iota(jnp.int32, shape, 0)
    full = lambda v: jnp.broadcast_to(v, shape)
    done = []
    for j in range(n // SUB):
        b = parts[j]
        base = j * SUB
        cols = [full(b[:, base + k : base + k + 1]) for k in range(SUB)]
        final = jnp.zeros(shape, jnp.float32)
        for k in range(SUB):
            pivot = full(cols[k][k : k + 1, :])
            inv = 1.0 / pivot
            root = lax.rsqrt(pivot)
            here = lane == base + k
            own = sub == k
            m = cols[k] * inv
            row = full(b[k : k + 1, :])
            past = jnp.where(lane < base + k, row * root, 0.0)
            final = jnp.where(own, jnp.where(here, root, past), final)
            for q in range(k + 1, SUB):
                c = full(cols[q][k : k + 1, :])
                cols[q] = jnp.where(own, c * inv, cols[q] - m * c)
            one = jnp.where(here, 1.0, row)
            b = jnp.where(own, one * inv, jnp.where(here, 0.0, b) - m * one)
        done.append(final)
        rows = [full(b[k : k + 1, :]) for k in range(SUB)]
        inside = (lane >= base) & (lane < base + SUB)
        for i in range(j + 1, n // SUB):
            t = [full(parts[i][:, base + k : base + k + 1]) * rows[k] for k in range(SUB)]
            t = ((t[0] + t[1]) + (t[2] + t[3])) + ((t[4] + t[5]) + (t[6] + t[7]))
            parts[i] = jnp.where(inside, 0.0, parts[i]) - t
    return jnp.concatenate(done, axis=0)


def inverse_factor(gram):
    n = gram.shape[0]
    half = n // 2
    r = lax.broadcasted_iota(jnp.int32, (n, n), 0)
    c = lax.broadcasted_iota(jnp.int32, (n, n), 1)
    diag = jnp.where(r == c, gram, 0.0)
    across = lax.rsqrt(jnp.sum(diag, axis=0, keepdims=True))
    down = lax.rsqrt(jnp.sum(diag, axis=1, keepdims=True))
    unit = jnp.where(r == c, 1.0, gram * across * down)
    first = block_inverse(unit[:half, :half])
    lower = dot(unit[half:, :half], first, HIGHEST, (1, 1))
    second = block_inverse(unit[half:, half:] - dot(lower, lower, HIGHEST, (1, 1)))
    corner = -dot(second, dot(lower, first, HIGHEST), HIGHEST)
    top = jnp.concatenate([first, jnp.zeros_like(first)], axis=1)
    return jnp.concatenate([top, jnp.concatenate([corner, second], axis=1)], axis=0) * across


def sketch_kernel(rows_ref, cols_ref, values_ref, test_ref, tile_ref, part_ref):
    count, width = values_ref.shape[0], values_ref.shape[1]
    tile_ref[...] = jnp.zeros_like(tile_ref)
    for n in range(count):
        row = pl.multiple_of(rows_ref[n] * width, width)
        col = pl.multiple_of(cols_ref[n] * width, width)
        tile_ref[pl.ds(row, width), pl.ds(col, width)] = values_ref[n]
    part_ref[...] = dot(tile_ref[...], test_ref[...]).reshape(part_ref.shape)


def cosketch_kernel(side_ref, tile_ref, sketch_ref, out_ref):
    sketch = sketch_ref[...]
    groups, _, half = out_ref.shape
    co = dot_terms(tile_ref[...], sketch, (0, 0))
    split = co.shape[0] // groups
    out_ref[:, :split, :] = co[:, :half].reshape(groups, split, half)
    out_ref[:, split : 2 * split, :] = co[:, half:].reshape(groups, split, half)
    chosen = jnp.where(side_ref[0] == 0, sketch[:, :half], sketch[:, half:])
    gram = dot(sketch, chosen, HIGHEST, (0, 0))
    out_ref[:, 2 * split :, :] = gram.reshape(groups, gram.shape[0] // groups, half)


def resketch_kernel(tile_ref, both_ref, part_ref, gram_ref):
    both = both_ref[...]
    side = tile_ref.shape[0]
    split = side // both.shape[0]
    left = both[:, :split, :].reshape(side, both.shape[2])
    right = both[:, split : 2 * split, :].reshape(side, both.shape[2])
    co = jnp.concatenate([left, right], axis=1)
    part_ref[...] = dot_terms(tile_ref[...], co).reshape(part_ref.shape)
    gram_ref[...] = both[:, 2 * split :, :].reshape(gram_ref.shape)


def factor_kernel(side_ref, own_ref, other_ref, out_ref):
    own, other = own_ref[...], other_ref[...]
    left = jnp.where(side_ref[0] == 0, own, other)
    right = jnp.where(side_ref[0] == 0, other, own)
    out_ref[...] = inverse_factor(jnp.concatenate([left, right], axis=1))


def gram_kernel(parts_ref, inverse_ref, share_ref, gram_ref):
    share = dot(jnp.sum(parts_ref[...], axis=0), inverse_ref[...], HIGHEST, (1, 1))
    share_ref[...] = share
    gram_ref[...] = dot(share, share, HIGHEST, (0, 0)).reshape(gram_ref.shape)


def final_kernel(scale, share_ref, gram_ref, out_ref):
    rank = out_ref.shape[1]
    inverse = inverse_factor(gram_ref[...].reshape(rank, rank))
    out_ref[...] = dot(share_ref[...], inverse, HIGHEST, (1, 1)) * scale


def to_each(x, axis):
    return lax.all_to_all(x, axis, 0, 0, tiled=True)


def from_each(x, axis):
    size = lax.axis_size(axis)
    return to_each(jnp.broadcast_to(x[None], (size,) + x.shape), axis)


def f32(*shape):
    return jax.ShapeDtypeStruct(shape, jnp.float32)


def per_device(block_values, block_rows, block_cols, test_matrix):
    values = block_values[0, 0]
    side, rank = test_matrix.shape
    half = rank // 2
    n_rows, n_feat = lax.axis_size("rows"), lax.axis_size("feat")
    scale = float(side * n_rows) ** 0.5
    share = side // n_feat
    core = (lax.axis_index("feat") % 2).astype(jnp.int32).reshape(1)

    tile, part = pl.pallas_call(
        sketch_kernel,
        in_specs=[SMEM, SMEM, VMEM, VMEM],
        out_specs=[VMEM, VMEM],
        out_shape=[jax.ShapeDtypeStruct((side, side), jnp.bfloat16), f32(n_feat, share, rank)],
    )(block_rows[0, 0], block_cols[0, 0], values, test_matrix)
    sketch = lax.all_gather(jnp.sum(to_each(part, "feat"), axis=0), "feat", axis=0, tiled=True)

    both = pl.pallas_call(
        cosketch_kernel,
        in_specs=[SMEM, VMEM, VMEM],
        out_specs=VMEM,
        out_shape=f32(n_rows, 2 * side // n_rows + rank // n_rows, half),
    )(core, tile, sketch)
    both = from_each(jnp.sum(to_each(both, "rows"), axis=0), "rows")

    part, own = pl.pallas_call(
        resketch_kernel,
        in_specs=[VMEM, VMEM],
        out_specs=[VMEM, VMEM],
        out_shape=[f32(n_feat, share, rank), f32(rank, half)],
    )(tile, both)
    parts = to_each(part, "feat")
    other = lax.ppermute(own, "feat", [(i, i ^ 1) for i in range(n_feat)])
    inverse = pl.pallas_call(
        factor_kernel,
        in_specs=[SMEM, VMEM, VMEM],
        out_specs=VMEM,
        out_shape=f32(rank, rank),
        cost_estimate=pl.CostEstimate(flops=10**10, bytes_accessed=10**6, transcendentals=0),
    )(core, own, other)

    resketch, gram = pl.pallas_call(
        gram_kernel,
        in_specs=[VMEM, VMEM],
        out_specs=[VMEM, VMEM],
        out_shape=[f32(share, rank), f32(n_rows, rank // n_rows, rank)],
    )(parts, inverse)
    gram = jnp.sum(to_each(gram, "rows"), axis=0)
    gram = jnp.sum(lax.all_gather(gram, "feat", axis=0), axis=0)
    return pl.pallas_call(
        lambda *refs: final_kernel(scale, *refs),
        in_specs=[VMEM, VMEM],
        out_specs=VMEM,
        out_shape=f32(share, rank),
    )(resketch, from_each(gram, "rows"))


def solution(mesh):
    placed = (
        P("rows", "feat", None, None, None),
        P("rows", "feat", None),
        P("rows", "feat", None),
        P("feat", None),
    )
    return jax.shard_map(
        per_device, mesh=mesh, in_specs=placed, out_specs=P(("rows", "feat"), None), check_vma=False
    )
```

time: 310 us -> 200 us (0.65)
  other arithmetic: 109 us -> 0.14 us
  Pallas kernels: 5.4 us -> 36.2 us
  waiting for transfers between devices: 37 us -> 21.5 us
  local copies, waits for them, and re-layouts: 9.97 us -> 1.5 us
  matrix products: 4.92 us -> 0 us
  blocking collectives: 120 us -> 116 us
  starting transfers between devices: 18.3 us -> 22.2 us
    another operation x18 -> x0, other arithmetic: 109 us -> none  [the longest x13 68.7 us: inverse_factor(): lower = jnp.linalg.cholesky(gram)]
    pallas_call x2 -> x6, Pallas kernels: 5.4 us -> 36.2 us  [the longest x1 12.7 us: per_device(): pl.pallas_call(lambda *refs: final_kernel(scale, *refs), in_specs=[VMEM,...]
    all_to_all x2, waiting for transfers between devices: 37 us -> 21.5 us  [to_each(): return lax.all_to_all(x, axis, 0, 0, tiled=True)]
    another operation x19 -> x0, local copies, waits for them, and re-layouts: 8.18 us -> none  [the longest x15 8.13 us: inverse_factor(): lax.linalg.triangular_solve(lower, identity, left_side=True, lower=True)]
    ppermute x0 -> x1, starting transfers between devices: none -> 6.84 us  [per_device(): other = lax.ppermute(own, 'feat', [(i, i ^ 1) for i in range(n_feat)])]
    all_to_all x4, blocking collectives: 87.6 us -> 83 us  [to_each(): return lax.all_to_all(x, axis, 0, 0, tiled=True)]
  transfers between devices with their start and end apart: 2 -> 3, of which waited for: 2 -> 2; matrix products, arithmetic and copies ran while one was open for 0% -> 0% of each run, Pallas kernels for 0% -> 6%
where the time goes in v2:
time: 200 us; the launch traced here: 197 us
  blocking collectives  116 us (58%)
  Pallas kernels  36.2 us (18%)
  starting transfers between devices  22.2 us (11%)
  waiting for transfers between devices  21.5 us (11%)
    all_to_all x4, blocking collectives, to_each(): return lax.all_to_all(x, axis, 0, 0, tiled=True)  83 us
    all_to_all x2, waiting for transfers between devices, to_each(): return lax.all_to_all(x, axis, 0, 0, tiled=True)  21.5 us
    all_gather x1, blocking collectives, per_device(): lax.all_gather(jnp.sum(to_each(part, 'feat'), axis=0), 'feat', axis=0, ti...  17.3 us
    all_gather x1, blocking collectives, per_device(): gram = jnp.sum(lax.all_gather(gram, 'feat', axis=0), axis=0)  15.4 us
    all_to_all x2, starting transfers between devices, to_each(): return lax.all_to_all(x, axis, 0, 0, tiled=True)  15.3 us
    pallas_call x1, Pallas kernels, per_device(): pl.pallas_call(lambda *refs: final_kernel(scale, *refs), in_specs=[VMEM,...  12.7 us
    pallas_call x1, Pallas kernels, per_device(): pl.pallas_call(factor_kernel, in_specs=[SMEM, VMEM, VMEM], out_specs=VMEM...  12.5 us
    ppermute x1, starting transfers between devices, per_device(): other = lax.ppermute(own, 'feat', [(i, i ^ 1) for i in range(n_feat)])  6.84 us
  transfers between devices with their start and end apart: 3, of which 2 were waited for; matrix products, arithmetic and copies ran while one was open for 0% of the time, Pallas kernels for 6%

profile of v2, /device:TPU:1, one launch (start us, length us, event | category | flops | bytes accessed | tf_op | source)
XLA Modules:
  0.0 197.3 jit_solution(17157091888770214873)
XLA Ops:
  0.0 2.2 %shard_map.46 = (bf16[512,512]{1,0:T(8,128)(2,1)}, f32[16,32,256]{2,1,0:T(8,128)}) custom-call(s32[12]{0:T(128)} %bitcast.7, s32[12]{0:T(128)} %bitcast.8, bf16[12,128,128]{2,1,0:T(8,128)(2,1)} %bitcast.6, bf16[512,256]{1,0:T(8,128)(2,1)} %test_ref.1), custom_call_target="tpu_custom_call" | custom-call | tf_op jit(solution)/shard_map/pallas_call | solution.py:161
  2.2 10.2 %all-to-all-start = ((f32[16,32,256]{2,1,0:T(8,128)}), f32[16,32,256]{2,1,0:T(8,128)S(1)}, u32[]{:S(2)}, u32[]{:S(2)}) async-start(f32[16,32,256]{2,1,0:T(8,128)} %get-tuple-element.12), calls=%async_computation | async-start | bytes 1048576 | tf_op jit(solution)/shard_map/all_to_all | solution.py:140
  12.5 17.3 %all-to-all-done = f32[16,32,256]{2,1,0:T(8,128)S(1)} async-done(((f32[16,32,256]{2,1,0:T(8,128)}), f32[16,32,256]{2,1,0:T(8,128)S(1)}, u32[]{:S(2)}, u32[]{:S(2)}) %all-to-all-start) | async-done | bytes 524320 | tf_op jit(solution)/shard_map/all_to_all | solution.py:140
  29.9 17.3 %all_gather.9.sketch_ref = f32[512,256]{1,0:T(8,128)} all-gather(f32[32,256]{1,0:T(8,128)S(1)} %reduce_sum.36), channel_id=1, replica_groups=mesh['rows'=32,'feat'=16] {'feat'}, dimensions={0}, use_global_device_ids=true | all-gather | bytes 557056 | tf_op jit(solution)/shard_map/all_gather | solution.py:167
  47.2 3.1 %shard_map.47 = f32[32,40,128]{2,1,0:T(8,128)} custom-call(s32[1]{0:T(128)} %bitcast.3.side_ref, bf16[512,512]{1,0:T(8,128)(2,1)} %get-tuple-element.11.tile_ref, f32[512,256]{1,0:T(8,128)} %all_gather.9.sketch_ref), custom_call_target="tpu_custom_call" | custom-call | tf_op jit(solution)/shard_map/pallas_call | solution.py:169
  50.3 28.0 %all_to_all.30 = f32[32,40,128]{2,1,0:T(8,128)S(1)} all-to-all(f32[32,40,128]{2,1,0:T(8,128)} %shard_map.47), channel_id=1, replica_groups=mesh['rows'=32,'feat'=16] {'rows'}, dimensions={0} | all-to-all | bytes 1310720 | tf_op jit(solution)/shard_map/all_to_all | solution.py:140
  78.3 0.1 reduce_sum.37
  78.4 24.8 %all_to_all.31.both_ref = f32[32,40,128]{2,1,0:T(8,128)} all-to-all(f32[32,40,128]{2,1,0:T(8,128)S(1)} %broadcast_in_dim.4), channel_id=1, replica_groups=mesh['rows'=32,'feat'=16] {'rows'}, dimensions={0} | all-to-all | bytes 1310720 | tf_op jit(solution)/shard_map/all_to_all | solution.py:140
  103.1 2.7 %shard_map.48 = (f32[16,32,256]{2,1,0:T(8,128)}, f32[256,128]{1,0:T(8,128)}) custom-call(bf16[512,512]{1,0:T(8,128)(2,1)} %get-tuple-element.11.tile_ref, f32[32,40,128]{2,1,0:T(8,128)} %all_to_all.31.both_ref), custom_call_target="tpu_custom_call" | custom-call | tf_op jit(solution)/shard_map/pallas_call | solution.py:177
  105.8 6.8 %collective-permute-start = (f32[256,128]{1,0:T(8,128)}, f32[256,128]{1,0:T(8,128)S(1)}, u32[]{:S(2)}, u32[]{:S(2)}) collective-permute-start(f32[256,128]{1,0:T(8,128)} %get-tuple-element.14.own_ref), channel_id=1, source_target_pairs={{0,1},{1,0},{2,3},{3,2},{4,5},{5,4},{6,7},{7,6},{8,9},{9,8},{10,11... | collective-permute-start | bytes 393224 | tf_op jit(solution)/shard_map/ppermute | solution.py:184
  112.6 5.1 %all-to-all-start.3 = ((f32[16,32,256]{2,1,0:T(8,128)}), f32[16,32,256]{2,1,0:T(8,128)S(1)}, u32[]{:S(2)}, u32[]{:S(2)}) async-start(f32[16,32,256]{2,1,0:T(8,128)} %get-tuple-element.13), calls=%async_computation.3 | async-start | bytes 1048576 | tf_op jit(solution)/shard_map/all_to_all | solution.py:140
  117.7 0.0 collective-permute-done.other_ref
  117.7 0.0 copy-start.1
  117.8 0.6 copy-done.1
  118.4 12.5 %shard_map.49.inverse_ref = f32[256,256]{1,0:T(8,128)} custom-call(s32[1]{0:T(128)} %bitcast.3.side_ref, f32[256,128]{1,0:T(8,128)} %get-tuple-element.14.own_ref, f32[256,128]{1,0:T(8,128)} %copy-done.1), custom_call_target="tpu_custom_call" | custom-call | flops 10000000000 | bytes 1000000 | tf_op jit(solution)/shard_map/pallas_call | solution.py:185
  130.9 4.2 %all-to-all-done.3.parts_ref = f32[16,32,256]{2,1,0:T(8,128)S(1)} async-done(((f32[16,32,256]{2,1,0:T(8,128)}), f32[16,32,256]{2,1,0:T(8,128)S(1)}, u32[]{:S(2)}, u32[]{:S(2)}) %all-to-all-start.3) | async-done | bytes 524320 | tf_op jit(solution)/shard_map/all_to_all | solution.py:140
  135.1 0.0 copy-start
  135.1 0.8 copy-done
  135.8 2.9 %shard_map.50 = (f32[32,256]{1,0:T(8,128)}, f32[32,8,256]{2,1,0:T(8,128)}) custom-call(f32[16,32,256]{2,1,0:T(8,128)} %copy-done, f32[256,256]{1,0:T(8,128)} %shard_map.49.inverse_ref), custom_call_target="tpu_custom_call" | custom-call | tf_op jit(solution)/shard_map/pallas_call | solution.py:193
  138.8 15.7 %all_to_all.32 = f32[32,8,256]{2,1,0:T(8,128)S(1)} all-to-all(f32[32,8,256]{2,1,0:T(8,128)} %get-tuple-element.16), channel_id=1, replica_groups=mesh['rows'=32,'feat'=16] {'rows'}, dimensions={0} | all-to-all | bytes 524288 | tf_op jit(solution)/shard_map/all_to_all | solution.py:140
  154.5 15.4 %all-gather = f32[128,256]{1,0:T(8,128)S(1)} all-gather(f32[8,256]{1,0:T(8,128)S(1)} %reduce_sum.38), channel_id=2, replica_groups=mesh['rows'=32,'feat'=16] {'feat'}, dimensions={0}, use_global_device_ids=true | all-gather | bytes 139264 | tf_op jit(solution)/shard_map/all_gather | solution.py:200
  170.0 14.5 %all_to_all.33.refs_1_ = f32[32,8,256]{2,1,0:T(8,128)} all-to-all(f32[32,8,256]{2,1,0:T(8,128)S(1)} %broadcast_in_dim.5), channel_id=1, replica_groups=mesh['rows'=32,'feat'=16] {'rows'}, dimensions={0} | all-to-all | bytes 524288 | tf_op jit(solution)/shard_map/all_to_all | solution.py:140
  184.5 12.7 %shard_map.51 = f32[32,256]{1,0:T(8,128)} custom-call(f32[32,256]{1,0:T(8,128)} %get-tuple-element.15.refs_0_, f32[32,8,256]{2,1,0:T(8,128)} %all_to_all.33.refs_1_), custom_call_target="tpu_custom_call" | custom-call | tf_op jit(solution)/shard_map/pallas_call | solution.py:201
  (5 shorter events, 0.2 us)
Async XLA Ops:
  2.2 27.6 %all-to-all-start = ((f32[16,32,256]{2,1,0:T(8,128)}), f32[16,32,256]{2,1,0:T(8,128)S(1)}, u32[]{:S(2)}, u32[]{:S(2)}) async-start(f32[16,32,256]{2,1,0:T(8,128)} %get-tuple-element.12), calls=%async_computation | async-start | bytes 1048576 | tf_op jit(solution)/shard_map/all_to_all | solution.py:140
  105.8 11.9 %collective-permute-start = (f32[256,128]{1,0:T(8,128)}, f32[256,128]{1,0:T(8,128)S(1)}, u32[]{:S(2)}, u32[]{:S(2)}) collective-permute-start(f32[256,128]{1,0:T(8,128)} %get-tuple-element.14.own_ref), channel_id=1, source_target_pairs={{0,1},{1,0},{2,3},{3,2},{4,5},{5,4},{6,7},{7,6},{8,9},{9,8},{10,11... | collective-permute-start | bytes 393224 | tf_op jit(solution)/shard_map/ppermute | solution.py:184
  112.6 22.4 %all-to-all-start.3 = ((f32[16,32,256]{2,1,0:T(8,128)}), f32[16,32,256]{2,1,0:T(8,128)S(1)}, u32[]{:S(2)}, u32[]{:S(2)}) async-start(f32[16,32,256]{2,1,0:T(8,128)} %get-tuple-element.13), calls=%async_computation.3 | async-start | bytes 1048576 | tf_op jit(solution)/shard_map/all_to_all | solution.py:140
  117.7 0.7 copy-start.1
  135.1 0.8 copy-start

commit v3 on v2

--- a/solution.py
+++ b/solution.py
@@ -6,6 +6,7 @@
 from jax.sharding import PartitionSpec as P
 
 HIGHEST = lax.Precision.HIGHEST
+PARAMS = pltpu.CompilerParams(vmem_limit_bytes=12 * 2**20)
 VMEM = pl.BlockSpec(memory_space=pltpu.VMEM)
 SMEM = pl.BlockSpec(memory_space=pltpu.SMEM)
 SUB = 8
@@ -38,30 +39,40 @@
     full = lambda v: jnp.broadcast_to(v, shape)
     done = []
     for j in range(n // SUB):
-        b = parts[j]
+        rows = parts[j]
         base = j * SUB
-        cols = [full(b[:, base + k : base + k + 1]) for k in range(SUB)]
+        cols = [full(rows[:, base + k : base + k + 1]) for k in range(SUB)]
         final = jnp.zeros(shape, jnp.float32)
-        for k in range(SUB):
-            pivot = full(cols[k][k : k + 1, :])
-            inv = 1.0 / pivot
-            root = lax.rsqrt(pivot)
-            here = lane == base + k
-            own = sub == k
-            m = cols[k] * inv
-            row = full(b[k : k + 1, :])
-            past = jnp.where(lane < base + k, row * root, 0.0)
-            final = jnp.where(own, jnp.where(here, root, past), final)
-            for q in range(k + 1, SUB):
-                c = full(cols[q][k : k + 1, :])
-                cols[q] = jnp.where(own, c * inv, cols[q] - m * c)
-            one = jnp.where(here, 1.0, row)
-            b = jnp.where(own, one * inv, jnp.where(here, 0.0, b) - m * one)
+        for k in range(0, SUB, 2):
+            a = full(cols[k][k : k + 1, :])
+            b = full(cols[k + 1][k : k + 1, :])
+            d = full(cols[k + 1][k + 1 : k + 2, :])
+            det = a * d - b * b
+            inv = 1.0 / det
+            first, second = sub == k, sub == k + 1
+            own = first | second
+            m1 = jnp.where(first, -1.0, jnp.where(second, 0.0, cols[k]))
+            m2 = jnp.where(second, -1.0, jnp.where(first, 0.0, cols[k + 1]))
+            w1 = m1 * d - m2 * b
+            w2 = m2 * a - m1 * b
+            for q in range(k + 2, SUB):
+                z = w1 * full(cols[q][k : k + 1, :]) + w2 * full(cols[q][k + 1 : k + 2, :])
+                cols[q] = jnp.where(own, 0.0, cols[q]) - z * inv
+            here, after = lane == base + k, lane == base + k + 1
+            r1 = jnp.where(here, 1.0, jnp.where(after, 0.0, full(rows[k : k + 1, :])))
+            r2 = jnp.where(after, 1.0, jnp.where(here, 0.0, full(rows[k + 1 : k + 2, :])))
+            root = lax.rsqrt(a)
+            inv_a = root * root
+            u1 = jnp.where(lane <= base + k, r1 * root, 0.0)
+            u2 = (r2 - (b * inv_a) * r1) * lax.rsqrt(det * inv_a)
+            u2 = jnp.where(lane <= base + k + 1, u2, 0.0)
+            final = jnp.where(first, u1, jnp.where(second, u2, final))
+            rows = jnp.where(own | here | after, 0.0, rows) - (w1 * r1 + w2 * r2) * inv
         done.append(final)
-        rows = [full(b[k : k + 1, :]) for k in range(SUB)]
+        pivots = [full(rows[k : k + 1, :]) for k in range(SUB)]
         inside = (lane >= base) & (lane < base + SUB)
         for i in range(j + 1, n // SUB):
-            t = [full(parts[i][:, base + k : base + k + 1]) * rows[k] for k in range(SUB)]
+            t = [full(parts[i][:, base + k : base + k + 1]) * pivots[k] for k in range(SUB)]
             t = ((t[0] + t[1]) + (t[2] + t[3])) + ((t[4] + t[5]) + (t[6] + t[7]))
             parts[i] = jnp.where(inside, 0.0, parts[i]) - t
     return jnp.concatenate(done, axis=0)
@@ -162,6 +173,7 @@
         sketch_kernel,
         in_specs=[SMEM, SMEM, VMEM, VMEM],
         out_specs=[VMEM, VMEM],
+        compiler_params=PARAMS,
         out_shape=[jax.ShapeDtypeStruct((side, side), jnp.bfloat16), f32(n_feat, share, rank)],
     )(block_rows[0, 0], block_cols[0, 0], values, test_matrix)
     sketch = lax.all_gather(jnp.sum(to_each(part, "feat"), axis=0), "feat", axis=0, tiled=True)
@@ -170,6 +182,7 @@
         cosketch_kernel,
         in_specs=[SMEM, VMEM, VMEM],
         out_specs=VMEM,
+        compiler_params=PARAMS,
         out_shape=f32(n_rows, 2 * side // n_rows + rank // n_rows, half),
     )(core, tile, sketch)
     both = from_each(jnp.sum(to_each(both, "rows"), axis=0), "rows")
@@ -178,6 +191,7 @@
         resketch_kernel,
         in_specs=[VMEM, VMEM],
         out_specs=[VMEM, VMEM],
+        compiler_params=PARAMS,
         out_shape=[f32(n_feat, share, rank), f32(rank, half)],
     )(tile, both)
     parts = to_each(part, "feat")
@@ -186,6 +200,7 @@
         factor_kernel,
         in_specs=[SMEM, VMEM, VMEM],
         out_specs=VMEM,
+        compiler_params=PARAMS,
         out_shape=f32(rank, rank),
         cost_estimate=pl.CostEstimate(flops=10**10, bytes_accessed=10**6, transcendentals=0),
     )(core, own, other)
@@ -194,14 +209,16 @@
         gram_kernel,
         in_specs=[VMEM, VMEM],
         out_specs=[VMEM, VMEM],
+        compiler_params=PARAMS,
         out_shape=[f32(share, rank), f32(n_rows, rank // n_rows, rank)],
     )(parts, inverse)
     gram = jnp.sum(to_each(gram, "rows"), axis=0)
-    gram = jnp.sum(lax.all_gather(gram, "feat", axis=0), axis=0)
+    gram = jnp.sum(from_each(gram, "feat"), axis=0)
     return pl.pallas_call(
         lambda *refs: final_kernel(scale, *refs),
         in_specs=[VMEM, VMEM],
         out_specs=VMEM,
+        compiler_params=PARAMS,
         out_shape=f32(share, rank),
     )(resketch, from_each(gram, "rows"))
 

time: 200 us -> 187 us (0.935); the launches traced: 197 us -> 186 us
  Pallas kernels: 36.2 us -> 22.6 us
  waiting for transfers between devices: 21.5 us -> 26.6 us
  blocking collectives: 116 us -> 112 us
    all_gather x1 -> x0, blocking collectives: 15.4 us -> none  [per_device(): gram = jnp.sum(lax.all_gather(gram, 'feat', axis=0), axis=0)]
    all_to_all x4 -> x5, blocking collectives: 83 us -> 96.1 us  [to_each(): return lax.all_to_all(x, axis, 0, 0, tiled=True)]
    all_to_all x2, waiting for transfers between devices: 21.5 us -> 26.6 us  [to_each(): return lax.all_to_all(x, axis, 0, 0, tiled=True)]
    pallas_call x1, Pallas kernels: 12.5 us -> 8.04 us  [per_device(): pl.pallas_call(factor_kernel, in_specs=[SMEM, VMEM, VMEM], out_specs=VMEM...]
    pallas_call x1, Pallas kernels: 12.7 us -> 9.25 us  [per_device(): pl.pallas_call(lambda *refs: final_kernel(scale, *refs), in_specs=[VMEM,...]
    pallas_call x1, Pallas kernels: 3.1 us -> 1.06 us  [per_device(): pl.pallas_call(cosketch_kernel, in_specs=[SMEM, VMEM, VMEM], out_specs=VM...]
  transfers between devices with their start and end apart: 3 -> 3, of which waited for: 2 -> 2; matrix products, arithmetic and copies ran while one was open for 0% -> 0% of each run, Pallas kernels for 6% -> 4%
where the time goes in v3:
time: 187 us; the launch traced here: 186 us
  blocking collectives  112 us (60%)
  waiting for transfers between devices  26.6 us (14%)
  Pallas kernels  22.6 us (12%)
  starting transfers between devices  22.2 us (12%)
  local copies, waits for them, and re-layouts  2.69 us (1%)
    all_to_all x5, blocking collectives, to_each(): return lax.all_to_all(x, axis, 0, 0, tiled=True)  96.1 us
    all_to_all x2, waiting for transfers between devices, to_each(): return lax.all_to_all(x, axis, 0, 0, tiled=True)  26.6 us
    all_gather x1, blocking collectives, per_device(): lax.all_gather(jnp.sum(to_each(part, 'feat'), axis=0), 'feat', axis=0, ti...  15.9 us
    all_to_all x2, starting transfers between devices, to_each(): return lax.all_to_all(x, axis, 0, 0, tiled=True)  15.3 us
    pallas_call x1, Pallas kernels, per_device(): pl.pallas_call(lambda *refs: final_kernel(scale, *refs), in_specs=[VMEM,...  9.25 us
    pallas_call x1, Pallas kernels, per_device(): pl.pallas_call(factor_kernel, in_specs=[SMEM, VMEM, VMEM], out_specs=VMEM...  8.04 us
    ppermute x1, starting transfers between devices, per_device(): other = lax.ppermute(own, 'feat', [(i, i ^ 1) for i in range(n_feat)])  6.84 us
  transfers between devices with their start and end apart: 3, of which 2 were waited for; matrix products, arithmetic and copies ran while one was open for 0% of the time, Pallas kernels for 4%

profile of v3, /device:TPU:1, one launch (start us, length us, event | category | flops | bytes accessed | tf_op | source)
XLA Modules:
  0.0 186.3 jit_solution(12519929565315024391)
XLA Ops:
  0.0 0.0 copy-start.2
  0.0 0.0 copy-start.3
  0.0 0.7 copy-done.2
  0.7 0.0 copy-done.3
  0.7 0.0 copy-start
  0.7 1.0 copy-done
  1.7 0.0 copy-start.1
  1.7 0.9 copy-done.1
  2.6 1.7 shard_map.46
  4.3 10.2 %all-to-all-start = ((f32[16,32,256]{2,1,0:T(8,128)}), f32[16,32,256]{2,1,0:T(8,128)S(1)}, u32[]{:S(2)}, u32[]{:S(2)}) async-start(f32[16,32,256]{2,1,0:T(8,128)} %get-tuple-element.12), calls=%async_computation | async-start | bytes 1048576 | tf_op jit(solution)/shard_map/all_to_all | solution.py:151
  14.6 17.3 %all-to-all-done = f32[16,32,256]{2,1,0:T(8,128)S(1)} async-done(((f32[16,32,256]{2,1,0:T(8,128)}), f32[16,32,256]{2,1,0:T(8,128)S(1)}, u32[]{:S(2)}, u32[]{:S(2)}) %all-to-all-start) | async-done | bytes 524320 | tf_op jit(solution)/shard_map/all_to_all | solution.py:151
  31.9 15.9 %all_gather.3.sketch_ref = f32[512,256]{1,0:T(8,128)S(1)} all-gather(f32[32,256]{1,0:T(8,128)S(1)} %reduce_sum.36), channel_id=1, replica_groups=mesh['rows'=32,'feat'=16] {'feat'}, dimensions={0}, use_global_device_ids=true | all-gather | bytes 557056 | tf_op jit(solution)/shard_map/all_gather | solution.py:179
  47.8 1.1 shard_map.47
  48.9 27.8 %all_to_all.35 = f32[32,40,128]{2,1,0:T(8,128)S(1)} all-to-all(f32[32,40,128]{2,1,0:T(8,128)S(1)} %shard_map.47), channel_id=1, replica_groups=mesh['rows'=32,'feat'=16] {'rows'}, dimensions={0} | all-to-all | bytes 1310720 | tf_op jit(solution)/shard_map/all_to_all | solution.py:151
  76.7 0.1 reduce_sum.37
  76.8 24.6 %all_to_all.36.both_ref = f32[32,40,128]{2,1,0:T(8,128)S(1)} all-to-all(f32[32,40,128]{2,1,0:T(8,128)S(1)} %broadcast_in_dim.6), channel_id=1, replica_groups=mesh['rows'=32,'feat'=16] {'rows'}, dimensions={0} | all-to-all | bytes 1310720 | tf_op jit(solution)/shard_map/all_to_all | solution.py:151
  101.4 1.4 shard_map.48
  102.9 6.8 %collective-permute-start = (f32[256,128]{1,0:T(8,128)S(1)}, f32[256,128]{1,0:T(8,128)S(1)}, u32[]{:S(2)}, u32[]{:S(2)}) collective-permute-start(f32[256,128]{1,0:T(8,128)S(1)} %get-tuple-element.14.own_ref), channel_id=1, source_target_pairs={{0,1},{1,0},{2,3},{3,2},{4,5},{5,4},{6,7},{7,6},{8,9},{9,8},{10,11... | collective-permute-start | bytes 393224 | tf_op jit(solution)/shard_map/ppermute | solution.py:198
  109.7 5.1 %all-to-all-start.3 = ((f32[16,32,256]{2,1,0:T(8,128)}), f32[16,32,256]{2,1,0:T(8,128)S(1)}, u32[]{:S(2)}, u32[]{:S(2)}) async-start(f32[16,32,256]{2,1,0:T(8,128)} %get-tuple-element.13), calls=%async_computation.3 | async-start | bytes 1048576 | tf_op jit(solution)/shard_map/all_to_all | solution.py:151
  114.8 0.0 collective-permute-done.other_ref
  114.8 8.0 %shard_map.49.inverse_ref = f32[256,256]{1,0:T(8,128)S(1)} custom-call(s32[1]{0:T(128)} %bitcast.3.side_ref, f32[256,128]{1,0:T(8,128)S(1)} %get-tuple-element.14.own_ref, f32[256,128]{1,0:T(8,128)S(1)} %collective-permute-done.other_ref), custom_call_target="tpu_custom_call" | custom-call | flops 10000000000 | bytes 1000000 | tf_op jit(solution)/shard_map/pallas_call | solution.py:199
  122.8 9.3 %all-to-all-done.3.parts_ref = f32[16,32,256]{2,1,0:T(8,128)S(1)} async-done(((f32[16,32,256]{2,1,0:T(8,128)}), f32[16,32,256]{2,1,0:T(8,128)S(1)}, u32[]{:S(2)}, u32[]{:S(2)}) %all-to-all-start.3) | async-done | bytes 524320 | tf_op jit(solution)/shard_map/all_to_all | solution.py:151
  132.1 1.1 shard_map.50
  133.2 15.5 %all_to_all.37 = f32[32,8,256]{2,1,0:T(8,128)S(1)} all-to-all(f32[32,8,256]{2,1,0:T(8,128)S(1)} %get-tuple-element.16), channel_id=1, replica_groups=mesh['rows'=32,'feat'=16] {'rows'}, dimensions={0} | all-to-all | bytes 524288 | tf_op jit(solution)/shard_map/all_to_all | solution.py:151
  148.8 13.6 %all_to_all.38 = f32[16,8,256]{2,1,0:T(8,128)S(1)} all-to-all(f32[16,8,256]{2,1,0:T(8,128)S(1)} %broadcast_in_dim.7), channel_id=1, replica_groups=mesh['rows'=32,'feat'=16] {'feat'}, dimensions={0} | all-to-all | bytes 262144 | tf_op jit(solution)/shard_map/all_to_all | solution.py:151
  162.4 14.6 %all_to_all.39.refs_1_ = f32[32,8,256]{2,1,0:T(8,128)S(1)} all-to-all(f32[32,8,256]{2,1,0:T(8,128)S(1)} %broadcast_in_dim.8), channel_id=1, replica_groups=mesh['rows'=32,'feat'=16] {'rows'}, dimensions={0} | all-to-all | bytes 524288 | tf_op jit(solution)/shard_map/all_to_all | solution.py:151
  177.1 9.2 %shard_map.51 = f32[32,256]{1,0:T(8,128)} custom-call(f32[32,256]{1,0:T(8,128)S(1)} %get-tuple-element.15.refs_0_, f32[32,8,256]{2,1,0:T(8,128)S(1)} %all_to_all.39.refs_1_), custom_call_target="tpu_custom_call" | custom-call | tf_op jit(solution)/shard_map/pallas_call | solution.py:217
  (6 shorter events, 0.2 us)
Async XLA Ops:
  0.0 0.7 copy-start.2
  0.0 0.7 copy-start.3
  0.7 1.0 copy-start
  1.7 0.9 copy-start.1
  4.3 27.6 %all-to-all-start = ((f32[16,32,256]{2,1,0:T(8,128)}), f32[16,32,256]{2,1,0:T(8,128)S(1)}, u32[]{:S(2)}, u32[]{:S(2)}) async-start(f32[16,32,256]{2,1,0:T(8,128)} %get-tuple-element.12), calls=%async_computation | async-start | bytes 1048576 | tf_op jit(solution)/shard_map/all_to_all | solution.py:151
  102.9 11.9 %collective-permute-start = (f32[256,128]{1,0:T(8,128)S(1)}, f32[256,128]{1,0:T(8,128)S(1)}, u32[]{:S(2)}, u32[]{:S(2)}) collective-permute-start(f32[256,128]{1,0:T(8,128)S(1)} %get-tuple-element.14.own_ref), channel_id=1, source_target_pairs={{0,1},{1,0},{2,3},{3,2},{4,5},{5,4},{6,7},{7,6},{8,9},{9,8},{10,11... | collective-permute-start | bytes 393224 | tf_op jit(solution)/shard_map/ppermute | solution.py:198
  109.7 22.4 %all-to-all-start.3 = ((f32[16,32,256]{2,1,0:T(8,128)}), f32[16,32,256]{2,1,0:T(8,128)S(1)}, u32[]{:S(2)}, u32[]{:S(2)}) async-start(f32[16,32,256]{2,1,0:T(8,128)} %get-tuple-element.13), calls=%async_computation.3 | async-start | bytes 1048576 | tf_op jit(solution)/shard_map/all_to_all | solution.py:151

commit v4 on v3

--- a/solution.py
+++ b/solution.py
@@ -3,10 +3,11 @@
 from jax import lax
 from jax.experimental import pallas as pl
 from jax.experimental.pallas import tpu as pltpu
-from jax.sharding import PartitionSpec as P
+from jax.sharding import Mesh, PartitionSpec as P
 
 HIGHEST = lax.Precision.HIGHEST
 PARAMS = pltpu.CompilerParams(vmem_limit_bytes=12 * 2**20)
+LARGE = pltpu.CompilerParams(vmem_limit_bytes=56 * 2**20)
 VMEM = pl.BlockSpec(memory_space=pltpu.VMEM)
 SMEM = pl.BlockSpec(memory_space=pltpu.SMEM)
 SUB = 8
@@ -95,44 +96,63 @@
     return jnp.concatenate([top, jnp.concatenate([corner, second], axis=1)], axis=0) * across
 
 
-def sketch_kernel(rows_ref, cols_ref, values_ref, test_ref, tile_ref, part_ref):
+def pick(core_ref, first, second):
+    return jnp.where(core_ref[0] == 0, first, second)
+
+
+def split_cores(core_ref, product, chips):
+    share = product.shape[0] // (2 * chips)
+    product = product.reshape(chips, 2, share, product.shape[1])
+    even, odd = product[:, 0], product[:, 1]
+    return pick(core_ref, even, odd), pick(core_ref, odd, even)
+
+
+def sketch_kernel(rows_ref, cols_ref, core_ref, values_ref, test_ref, tile_ref, keep_ref, send_ref):
     count, width = values_ref.shape[0], values_ref.shape[1]
     tile_ref[...] = jnp.zeros_like(tile_ref)
     for n in range(count):
         row = pl.multiple_of(rows_ref[n] * width, width)
         col = pl.multiple_of(cols_ref[n] * width, width)
         tile_ref[pl.ds(row, width), pl.ds(col, width)] = values_ref[n]
-    part_ref[...] = dot(tile_ref[...], test_ref[...]).reshape(part_ref.shape)
-
-
-def cosketch_kernel(side_ref, tile_ref, sketch_ref, out_ref):
+    product = dot(tile_ref[...], test_ref[...])
+    keep_ref[...], send_ref[...] = split_cores(core_ref, product, keep_ref.shape[0])
+
+
+def cosketch_kernel(core_ref, tile_ref, sketch_ref, out_ref):
     sketch = sketch_ref[...]
     groups, _, half = out_ref.shape
     co = dot_terms(tile_ref[...], sketch, (0, 0))
     split = co.shape[0] // groups
     out_ref[:, :split, :] = co[:, :half].reshape(groups, split, half)
     out_ref[:, split : 2 * split, :] = co[:, half:].reshape(groups, split, half)
-    chosen = jnp.where(side_ref[0] == 0, sketch[:, :half], sketch[:, half:])
+    chosen = pick(core_ref, sketch[:, :half], sketch[:, half:])
     gram = dot(sketch, chosen, HIGHEST, (0, 0))
     out_ref[:, 2 * split :, :] = gram.reshape(groups, gram.shape[0] // groups, half)
 
 
-def resketch_kernel(tile_ref, both_ref, part_ref, gram_ref):
+def resketch_kernel(core_ref, tile_ref, both_ref, keep_ref, send_ref, gram_ref):
     both = both_ref[...]
     side = tile_ref.shape[0]
+    chips, share, rank = keep_ref.shape
+    half = rank // 2
     split = side // both.shape[0]
-    left = both[:, :split, :].reshape(side, both.shape[2])
-    right = both[:, split : 2 * split, :].reshape(side, both.shape[2])
-    co = jnp.concatenate([left, right], axis=1)
-    part_ref[...] = dot_terms(tile_ref[...], co).reshape(part_ref.shape)
-    gram_ref[...] = both[:, 2 * split :, :].reshape(gram_ref.shape)
-
-
-def factor_kernel(side_ref, own_ref, other_ref, out_ref):
-    own, other = own_ref[...], other_ref[...]
-    left = jnp.where(side_ref[0] == 0, own, other)
-    right = jnp.where(side_ref[0] == 0, other, own)
-    out_ref[...] = inverse_factor(jnp.concatenate([left, right], axis=1))
+    left = both[:, :split, :].reshape(side, half)
+    right = both[:, split : 2 * split, :].reshape(side, half)
+    product = dot_terms(tile_ref[...], jnp.concatenate([left, right], axis=1))
+    keep_ref[...], send_ref[:, :share, :] = split_cores(core_ref, product, chips)
+    gram = both[:, 2 * split :, :].reshape(rank, half)
+    gram_ref[...] = gram
+    wide = jnp.concatenate([gram[:half], gram[half:]], axis=1)
+    send_ref[:, share:, :] = wide.reshape(chips, half // chips, rank)
+
+
+def factor_kernel(core_ref, own_ref, received_ref, out_ref):
+    rank, half = own_ref.shape
+    share = received_ref.shape[1] - half // received_ref.shape[0]
+    wide = received_ref[:, share:, :].reshape(half, rank)
+    own, other = own_ref[...], jnp.concatenate([wide[:, :half], wide[:, half:]], axis=0)
+    gram = jnp.concatenate([pick(core_ref, own, other), pick(core_ref, other, own)], axis=1)
+    out_ref[...] = inverse_factor(gram)
 
 
 def gram_kernel(parts_ref, inverse_ref, share_ref, gram_ref):
@@ -147,6 +167,9 @@
     out_ref[...] = dot(share_ref[...], inverse, HIGHEST, (1, 1)) * scale
 
 
+FEAT = ("y", "core")
+
+
 def to_each(x, axis):
     return lax.all_to_all(x, axis, 0, 0, tiled=True)
 
@@ -154,6 +177,10 @@
 def from_each(x, axis):
     size = lax.axis_size(axis)
     return to_each(jnp.broadcast_to(x[None], (size,) + x.shape), axis)
+
+
+def swap_cores(x):
+    return lax.ppermute(x, "core", [(0, 1), (1, 0)])
 
 
 def f32(*shape):
@@ -164,72 +191,75 @@
     values = block_values[0, 0]
     side, rank = test_matrix.shape
     half = rank // 2
-    n_rows, n_feat = lax.axis_size("rows"), lax.axis_size("feat")
+    n_rows, chips = lax.axis_size("rows"), lax.axis_size("y")
     scale = float(side * n_rows) ** 0.5
-    share = side // n_feat
-    core = (lax.axis_index("feat") % 2).astype(jnp.int32).reshape(1)
-
-    tile, part = pl.pallas_call(
+    share = side // (2 * chips)
+    core = lax.axis_index("core").astype(jnp.int32).reshape(1)
+
+    tile, keep, send = pl.pallas_call(
         sketch_kernel,
-        in_specs=[SMEM, SMEM, VMEM, VMEM],
-        out_specs=[VMEM, VMEM],
-        compiler_params=PARAMS,
-        out_shape=[jax.ShapeDtypeStruct((side, side), jnp.bfloat16), f32(n_feat, share, rank)],
-    )(block_rows[0, 0], block_cols[0, 0], values, test_matrix)
-    sketch = lax.all_gather(jnp.sum(to_each(part, "feat"), axis=0), "feat", axis=0, tiled=True)
+        in_specs=[SMEM, SMEM, SMEM, VMEM, VMEM],
+        out_specs=[VMEM] * 3,
+        out_shape=[jax.ShapeDtypeStruct((side, side), jnp.bfloat16)] + [f32(chips, share, rank)] * 2,
+        compiler_params=LARGE,
+    )(block_rows[0, 0], block_cols[0, 0], core, values, test_matrix)
+    sketch = jnp.sum(to_each(keep + swap_cores(send), "y"), axis=0)
+    sketch = lax.all_gather(sketch, FEAT, axis=0, tiled=True)
 
     both = pl.pallas_call(
         cosketch_kernel,
         in_specs=[SMEM, VMEM, VMEM],
         out_specs=VMEM,
-        compiler_params=PARAMS,
         out_shape=f32(n_rows, 2 * side // n_rows + rank // n_rows, half),
+        compiler_params=PARAMS,
     )(core, tile, sketch)
     both = from_each(jnp.sum(to_each(both, "rows"), axis=0), "rows")
 
-    part, own = pl.pallas_call(
+    keep, send, own = pl.pallas_call(
         resketch_kernel,
-        in_specs=[VMEM, VMEM],
-        out_specs=[VMEM, VMEM],
-        compiler_params=PARAMS,
-        out_shape=[f32(n_feat, share, rank), f32(rank, half)],
-    )(tile, both)
-    parts = to_each(part, "feat")
-    other = lax.ppermute(own, "feat", [(i, i ^ 1) for i in range(n_feat)])
+        in_specs=[SMEM, VMEM, VMEM],
+        out_specs=[VMEM] * 3,
+        out_shape=[f32(chips, share, rank), f32(chips, share + half // chips, rank), f32(rank, half)],
+        compiler_params=PARAMS,
+    )(core, tile, both)
+    received = swap_cores(send)
+    parts = to_each(keep + received[:, :share], "y")
     inverse = pl.pallas_call(
         factor_kernel,
         in_specs=[SMEM, VMEM, VMEM],
         out_specs=VMEM,
-        compiler_params=PARAMS,
         out_shape=f32(rank, rank),
+        compiler_params=PARAMS,
         cost_estimate=pl.CostEstimate(flops=10**10, bytes_accessed=10**6, transcendentals=0),
-    )(core, own, other)
+    )(core, own, received)
 
     resketch, gram = pl.pallas_call(
         gram_kernel,
-        in_specs=[VMEM, VMEM],
-        out_specs=[VMEM, VMEM],
-        compiler_params=PARAMS,
+        in_specs=[VMEM] * 2,
+        out_specs=[VMEM] * 2,
         out_shape=[f32(share, rank), f32(n_rows, rank // n_rows, rank)],
+        compiler_params=PARAMS,
     )(parts, inverse)
     gram = jnp.sum(to_each(gram, "rows"), axis=0)
-    gram = jnp.sum(from_each(gram, "feat"), axis=0)
+    gram = jnp.sum(from_each(gram, FEAT), axis=0)
     return pl.pallas_call(
         lambda *refs: final_kernel(scale, *refs),
-        in_specs=[VMEM, VMEM],
+        in_specs=[VMEM] * 2,
         out_specs=VMEM,
-        compiler_params=PARAMS,
         out_shape=f32(share, rank),
+        compiler_params=PARAMS,
     )(resketch, from_each(gram, "rows"))
 
 
 def solution(mesh):
+    n_rows, n_feat = mesh.devices.shape
+    chips = Mesh(mesh.devices.reshape(n_rows, n_feat // 2, 2), ("rows",) + FEAT)
     placed = (
-        P("rows", "feat", None, None, None),
-        P("rows", "feat", None),
-        P("rows", "feat", None),
-        P("feat", None),
+        P("rows", FEAT, None, None, None),
+        P("rows", FEAT, None),
+        P("rows", FEAT, None),
+        P(FEAT, None),
     )
     return jax.shard_map(
-        per_device, mesh=mesh, in_specs=placed, out_specs=P(("rows", "feat"), None), check_vma=False
+        per_device, mesh=chips, in_specs=placed, out_specs=P(("rows",) + FEAT, None), check_vma=False
     )

time: 187 us -> 179 us (0.957)
  waiting for transfers between devices: 26.6 us -> 5.67 us
  blocking collectives: 112 us -> 129 us
  starting transfers between devices: 22.2 us -> 19 us
  local copies, waits for them, and re-layouts: 2.69 us -> 0.08 us
    all_to_all x2 -> x1, waiting for transfers between devices: 26.6 us -> 2.99 us  [to_each(): return lax.all_to_all(x, axis, 0, 0, tiled=True)]
    all_to_all x5 -> x6, blocking collectives: 96.1 us -> 113 us  [to_each(): return lax.all_to_all(x, axis, 0, 0, tiled=True)]
    all_to_all x2 -> x1, starting transfers between devices: 15.3 us -> 3.41 us  [to_each(): return lax.all_to_all(x, axis, 0, 0, tiled=True)]
    ppermute x1 -> x2, starting transfers between devices: 6.84 us -> 15.6 us  [swap_cores(): return lax.ppermute(x, 'core', [(0, 1), (1, 0)])]
    ppermute x1 -> x2, waiting for transfers between devices: 0.01 us -> 2.68 us  [swap_cores(): return lax.ppermute(x, 'core', [(0, 1), (1, 0)])]
    unnamed x8 -> x2, local copies, waits for them, and re-layouts: 2.61 us -> 0.01 us
  transfers between devices with their start and end apart: 3 -> 3, of which waited for: 2 -> 3; matrix products, arithmetic and copies ran while one was open for 0% -> 0% of each run, Pallas kernels for 4% -> 5%
where the time goes in v4:
time: 179 us; the launch traced here: 178 us
  blocking collectives  129 us (72%)
  Pallas kernels  22.4 us (13%)
  starting transfers between devices  19 us (11%)
  waiting for transfers between devices  5.67 us (3%)
  other arithmetic  1.85 us (1%)
    all_to_all x6, blocking collectives, to_each(): return lax.all_to_all(x, axis, 0, 0, tiled=True)  113 us
    all_gather x1, blocking collectives, per_device(): sketch = lax.all_gather(sketch, FEAT, axis=0, tiled=True)  16.6 us
    ppermute x2, starting transfers between devices, swap_cores(): return lax.ppermute(x, 'core', [(0, 1), (1, 0)])  15.6 us
    pallas_call x1, Pallas kernels, per_device(): pl.pallas_call(lambda *refs: final_kernel(scale, *refs), in_specs=[VMEM]...  9.24 us
    pallas_call x1, Pallas kernels, per_device(): pl.pallas_call(factor_kernel, in_specs=[SMEM, VMEM, VMEM], out_specs=VMEM...  8.04 us
  transfers between devices with their start and end apart: 3, of which 3 were waited for; matrix products, arithmetic and copies ran while one was open for 0% of the time, Pallas kernels for 5%

profile of v4, /device:TPU:1, one launch (start us, length us, event | category | flops | bytes accessed | tf_op | source)
XLA Modules:
  0.0 178.4 jit_solution(11882773084055177147)
XLA Ops:
  0.0 2.3 %shard_map.46 = (bf16[512,512]{1,0:T(8,128)(2,1)}, f32[8,32,256]{2,1,0:T(8,128)}, f32[8,32,256]{2,1,0:T(8,128)}) custom-call(s32[12]{0:T(128)} %bitcast.5, s32[12]{0:T(128)} %bitcast.6, s32[1]{0:T(128)} %bitcast.core_ref, bf16[12,128,128]{2,1,0:T(8,128)(2,1)} %bitcast.4, bf16[512,256]{1,0:T(8,128)(2,1)} %test_ref.1), custom_call_target="tpu_custom_call" | custom-call | tf_op jit(solution)/shard_map/pallas_call | solution.py:199
  2.3 8.8 %collective-permute-start = (f32[8,32,256]{2,1,0:T(8,128)}, f32[8,32,256]{2,1,0:T(8,128)S(1)}, u32[]{:S(2)}, u32[]{:S(2)}) collective-permute-start(f32[8,32,256]{2,1,0:T(8,128)} %get-tuple-element.15), channel_id=1, source_target_pairs={{0,1},{1,0},{2,3},{3,2},{4,5},{5,4},{6,7},{7,6},{8,9},{9,8},{10,11... | collective-permute-start | bytes 786440 | tf_op jit(solution)/shard_map/ppermute | solution.py:183
  11.0 1.4 collective-permute-done
  12.4 1.0 add.6
  13.4 14.8 %all_to_all.35 = f32[8,32,256]{2,1,0:T(8,128)S(1)} all-to-all(f32[8,32,256]{2,1,0:T(8,128)S(1)} %add.6), channel_id=1, replica_groups=mesh['rows'=32,'y'=8,'core'=2] {'y'}, dimensions={0} | all-to-all | bytes 524288 | tf_op jit(solution)/shard_map/all_to_all | solution.py:174
  28.1 0.0 copy-start
  28.2 16.6 %all_gather.3.sketch_ref = f32[512,256]{1,0:T(8,128)S(1)} all-gather(f32[32,256]{1,0:T(8,128)S(1)} %reduce_sum.36), channel_id=1, replica_groups=mesh['rows'=32,'y'=8,'core'=2] {'y','core'}, dimensions={0}, use_global_device_ids=true | all-gather | bytes 557056 | tf_op jit(solution)/shard_map/all_gather | solution.py:207
  44.7 0.0 copy-done
  44.7 1.1 shard_map.47
  45.8 28.3 %all_to_all.36 = f32[32,40,128]{2,1,0:T(8,128)S(1)} all-to-all(f32[32,40,128]{2,1,0:T(8,128)S(1)} %shard_map.47), channel_id=1, replica_groups=mesh['rows'=32,'y'=8,'core'=2] {'rows'}, dimensions={0} | all-to-all | bytes 1310720 | tf_op jit(solution)/shard_map/all_to_all | solution.py:174
  74.1 0.1 reduce_sum.37
  74.2 24.6 %all_to_all.37.both_ref = f32[32,40,128]{2,1,0:T(8,128)S(1)} all-to-all(f32[32,40,128]{2,1,0:T(8,128)S(1)} %broadcast_in_dim.6), channel_id=1, replica_groups=mesh['rows'=32,'y'=8,'core'=2] {'rows'}, dimensions={0} | all-to-all | bytes 1310720 | tf_op jit(solution)/shard_map/all_to_all | solution.py:174
  98.8 0.6 shard_map.48
  99.5 6.9 %collective-permute-start.1 = (f32[8,48,256]{2,1,0:T(8,128)S(1)}, f32[8,48,256]{2,1,0:T(8,128)S(1)}, u32[]{:S(2)}, u32[]{:S(2)}) collective-permute-start(f32[8,48,256]{2,1,0:T(8,128)S(1)} %get-tuple-element.17), channel_id=1, source_target_pairs={{0,1},{1,0},{2,3},{3,2},{4,5},{5,4},{6,7},{7,6},{8,9},{9,8},{10,11... | collective-permute-start | bytes 1179656 | tf_op jit(solution)/shard_map/ppermute | solution.py:183
  106.3 1.3 collective-permute-done.1.received_ref
  107.7 0.7 slice_add_fusion
  108.4 3.4 %all-to-all-start.3 = ((f32[8,32,256]{2,1,0:T(8,128)}), f32[8,32,256]{2,1,0:T(8,128)S(1)}, u32[]{:S(2)}, u32[]{:S(2)}) async-start(f32[8,32,256]{2,1,0:T(8,128)} %slice_add_fusion), calls=%async_computation.3 | async-start | bytes 524288 | tf_op jit(solution)/shard_map/all_to_all | solution.py:174
  111.8 8.0 %shard_map.49.inverse_ref = f32[256,256]{1,0:T(8,128)S(1)} custom-call(s32[1]{0:T(128)} %bitcast.core_ref, f32[256,128]{1,0:T(8,128)S(1)} %get-tuple-element.18.own_ref, f32[8,48,256]{2,1,0:T(8,128)S(1)} %collective-permute-done.1.received_ref), custom_call_target="tpu_custom_call" | custom-call | flops 10000000000 | bytes 1000000 | tf_op jit(solution)/shard_map/pallas_call | solution.py:227
  119.9 3.0 %all-to-all-done.3.parts_ref = f32[8,32,256]{2,1,0:T(8,128)S(1)} async-done(((f32[8,32,256]{2,1,0:T(8,128)}), f32[8,32,256]{2,1,0:T(8,128)S(1)}, u32[]{:S(2)}, u32[]{:S(2)}) %all-to-all-start.3) | async-done | bytes 262176 | tf_op jit(solution)/shard_map/all_to_all | solution.py:174
  122.9 1.1 shard_map.50
  124.0 13.9 %all_to_all.38 = f32[32,8,256]{2,1,0:T(8,128)S(1)} all-to-all(f32[32,8,256]{2,1,0:T(8,128)S(1)} %get-tuple-element.20), channel_id=1, replica_groups=mesh['rows'=32,'y'=8,'core'=2] {'rows'}, dimensions={0} | all-to-all | bytes 524288 | tf_op jit(solution)/shard_map/all_to_all | solution.py:174
  137.9 16.4 %all_to_all.39 = f32[16,8,256]{2,1,0:T(8,128)S(1)} all-to-all(f32[16,8,256]{2,1,0:T(8,128)S(1)} %broadcast_in_dim.7), channel_id=1, replica_groups=mesh['rows'=32,'y'=8,'core'=2] {'y','core'}, dimensions={0} | all-to-all | bytes 262144 | tf_op jit(solution)/shard_map/all_to_all | solution.py:174
  154.4 14.8 %all_to_all.40.refs_1_ = f32[32,8,256]{2,1,0:T(8,128)S(1)} all-to-all(f32[32,8,256]{2,1,0:T(8,128)S(1)} %broadcast_in_dim.8), channel_id=1, replica_groups=mesh['rows'=32,'y'=8,'core'=2] {'rows'}, dimensions={0} | all-to-all | bytes 524288 | tf_op jit(solution)/shard_map/all_to_all | solution.py:174
  169.2 9.2 %shard_map.51 = f32[32,256]{1,0:T(8,128)} custom-call(f32[32,256]{1,0:T(8,128)S(1)} %get-tuple-element.19.refs_0_, f32[32,8,256]{2,1,0:T(8,128)S(1)} %all_to_all.40.refs_1_), custom_call_target="tpu_custom_call" | custom-call | tf_op jit(solution)/shard_map/pallas_call | solution.py:245
  (6 shorter events, 0.2 us)
Async XLA Ops:
  2.3 10.1 %collective-permute-start = (f32[8,32,256]{2,1,0:T(8,128)}, f32[8,32,256]{2,1,0:T(8,128)S(1)}, u32[]{:S(2)}, u32[]{:S(2)}) collective-permute-start(f32[8,32,256]{2,1,0:T(8,128)} %get-tuple-element.15), channel_id=1, source_target_pairs={{0,1},{1,0},{2,3},{3,2},{4,5},{5,4},{6,7},{7,6},{8,9},{9,8},{10,11... | collective-permute-start | bytes 786440 | tf_op jit(solution)/shard_map/ppermute | solution.py:183
  28.1 16.6 %copy-start = (bf16[512,512]{1,0:T(8,128)(2,1)S(1)}, bf16[512,512]{1,0:T(8,128)(2,1)}, u32[]{:S(2)}) copy-start(bf16[512,512]{1,0:T(8,128)(2,1)} %get-tuple-element.13.tile_ref) | copy-start | bytes 1572868
  99.5 8.2 %collective-permute-start.1 = (f32[8,48,256]{2,1,0:T(8,128)S(1)}, f32[8,48,256]{2,1,0:T(8,128)S(1)}, u32[]{:S(2)}, u32[]{:S(2)}) collective-permute-start(f32[8,48,256]{2,1,0:T(8,128)S(1)} %get-tuple-element.17), channel_id=1, source_target_pairs={{0,1},{1,0},{2,3},{3,2},{4,5},{5,4},{6,7},{7,6},{8,9},{9,8},{10,11... | collective-permute-start | bytes 1179656 | tf_op jit(solution)/shard_map/ppermute | solution.py:183
  108.4 14.5 %all-to-all-start.3 = ((f32[8,32,256]{2,1,0:T(8,128)}), f32[8,32,256]{2,1,0:T(8,128)S(1)}, u32[]{:S(2)}, u32[]{:S(2)}) async-start(f32[8,32,256]{2,1,0:T(8,128)} %slice_add_fusion), calls=%async_computation.3 | async-start | bytes 524288 | tf_op jit(solution)/shard_map/all_to_all | solution.py:174

commit v5 on v4

--- a/solution.py
+++ b/solution.py
@@ -10,7 +10,7 @@
 LARGE = pltpu.CompilerParams(vmem_limit_bytes=56 * 2**20)
 VMEM = pl.BlockSpec(memory_space=pltpu.VMEM)
 SMEM = pl.BlockSpec(memory_space=pltpu.SMEM)
-SUB = 8
+SUB = 16
 
 
 def dot(a, b, precision=None, contract=(1, 0)):
@@ -71,15 +71,25 @@
             rows = jnp.where(own | here | after, 0.0, rows) - (w1 * r1 + w2 * r2) * inv
         done.append(final)
         pivots = [full(rows[k : k + 1, :]) for k in range(SUB)]
-        inside = (lane >= base) & (lane < base + SUB)
-        for i in range(j + 1, n // SUB):
-            t = [full(parts[i][:, base + k : base + k + 1]) * pivots[k] for k in range(SUB)]
-            t = ((t[0] + t[1]) + (t[2] + t[3])) + ((t[4] + t[5]) + (t[6] + t[7]))
-            parts[i] = jnp.where(inside, 0.0, parts[i]) - t
+        if j + 1 < n // SUB:
+            t = [full(parts[j + 1][:, base + k : base + k + 1]) * pivots[k] for k in range(SUB)]
+            while len(t) > 1:
+                t = [t[i] + t[i + 1] for i in range(0, len(t), 2)]
+            inside = (lane >= base) & (lane < base + SUB)
+            parts[j + 1] = jnp.where(inside, 0.0, parts[j + 1]) - t[0]
+        if j + 2 < n // SUB:
+            rest = jnp.concatenate(parts[j + 2 :], axis=0)
+            spread = [jnp.zeros((base, n), jnp.float32)] if base else []
+            spread += [rows, jnp.zeros((n - base - SUB, n), jnp.float32)]
+            wide = lax.broadcasted_iota(jnp.int32, rest.shape, 1)
+            inside = (wide >= base) & (wide < base + SUB)
+            change = dot(jnp.where(inside, rest, 0.0), jnp.concatenate(spread, axis=0), HIGHEST)
+            rest = jnp.where(inside, 0.0, rest) - change
+            parts[j + 2 :] = [rest[i : i + SUB] for i in range(0, rest.shape[0], SUB)]
     return jnp.concatenate(done, axis=0)
 
 
-def inverse_factor(gram):
+def factor(gram):
     n = gram.shape[0]
     half = n // 2
     r = lax.broadcasted_iota(jnp.int32, (n, n), 0)
@@ -91,9 +101,23 @@
     first = block_inverse(unit[:half, :half])
     lower = dot(unit[half:, :half], first, HIGHEST, (1, 1))
     second = block_inverse(unit[half:, half:] - dot(lower, lower, HIGHEST, (1, 1)))
+    return across, first, lower, second
+
+
+def inverse_factor(gram):
+    across, first, lower, second = factor(gram)
     corner = -dot(second, dot(lower, first, HIGHEST), HIGHEST)
     top = jnp.concatenate([first, jnp.zeros_like(first)], axis=1)
     return jnp.concatenate([top, jnp.concatenate([corner, second], axis=1)], axis=0) * across
+
+
+def whiten(x, gram):
+    across, first, lower, second = factor(gram)
+    half = first.shape[0]
+    x = x * across
+    left = dot(x[:, :half], first, HIGHEST, (1, 1))
+    right = dot(x[:, half:] - dot(left, lower, HIGHEST, (1, 1)), second, HIGHEST, (1, 1))
+    return jnp.concatenate([left, right], axis=1)
 
 
 def pick(core_ref, first, second):
@@ -163,8 +187,7 @@
 
 def final_kernel(scale, share_ref, gram_ref, out_ref):
     rank = out_ref.shape[1]
-    inverse = inverse_factor(gram_ref[...].reshape(rank, rank))
-    out_ref[...] = dot(share_ref[...], inverse, HIGHEST, (1, 1)) * scale
+    out_ref[...] = whiten(share_ref[...], gram_ref[...].reshape(rank, rank)) * scale
 
 
 FEAT = ("y", "core")

time: 179 us -> 176 us (0.983)
  Pallas kernels: 22.4 us -> 18 us
  waiting for transfers between devices: 5.67 us -> 7.57 us
    pallas_call x1, Pallas kernels: 9.24 us -> 6.79 us  [per_device(): pl.pallas_call(lambda *refs: final_kernel(scale, *refs), in_specs=[VMEM]...]
    pallas_call x1, Pallas kernels: 8.04 us -> 6.14 us  [per_device(): pl.pallas_call(factor_kernel, in_specs=[SMEM, VMEM, VMEM], out_specs=VMEM...]
    all_to_all x1, waiting for transfers between devices: 2.99 us -> 4.89 us  [to_each(): return lax.all_to_all(x, axis, 0, 0, tiled=True)]
  transfers between devices with their start and end apart: 3 -> 3, of which waited for: 3 -> 3; matrix products, arithmetic and copies ran while one was open for 0% -> 0% of each run, Pallas kernels for 5% -> 4%
where the time goes in v5:
time: 176 us; the launch traced here: 175 us
  blocking collectives  128 us (73%)
  starting transfers between devices  19 us (11%)
  Pallas kernels  18 us (10%)
  waiting for transfers between devices  7.57 us (4%)
  other arithmetic  1.85 us (1%)
    all_to_all x6, blocking collectives, to_each(): return lax.all_to_all(x, axis, 0, 0, tiled=True)  112 us
    all_gather x1, blocking collectives, per_device(): sketch = lax.all_gather(sketch, FEAT, axis=0, tiled=True)  16.6 us
    ppermute x2, starting transfers between devices, swap_cores(): return lax.ppermute(x, 'core', [(0, 1), (1, 0)])  15.6 us
    pallas_call x1, Pallas kernels, per_device(): pl.pallas_call(lambda *refs: final_kernel(scale, *refs), in_specs=[VMEM]...  6.79 us
    pallas_call x1, Pallas kernels, per_device(): pl.pallas_call(factor_kernel, in_specs=[SMEM, VMEM, VMEM], out_specs=VMEM...  6.14 us
    all_to_all x1, waiting for transfers between devices, to_each(): return lax.all_to_all(x, axis, 0, 0, tiled=True)  4.89 us
  transfers between devices with their start and end apart: 3, of which 3 were waited for; matrix products, arithmetic and copies ran while one was open for 0% of the time, Pallas kernels for 4%

profile of v5, /device:TPU:1, one launch (start us, length us, event | category | flops | bytes accessed | tf_op | source)
XLA Modules:
  0.0 174.8 jit_solution(4875528121439130809)
XLA Ops:
  0.0 2.3 %shard_map.46 = (bf16[512,512]{1,0:T(8,128)(2,1)}, f32[8,32,256]{2,1,0:T(8,128)}, f32[8,32,256]{2,1,0:T(8,128)}) custom-call(s32[12]{0:T(128)} %bitcast.5, s32[12]{0:T(128)} %bitcast.6, s32[1]{0:T(128)} %bitcast.core_ref, bf16[12,128,128]{2,1,0:T(8,128)(2,1)} %bitcast.4, bf16[512,256]{1,0:T(8,128)(2,1)} %test_ref.1), custom_call_target="tpu_custom_call" | custom-call | tf_op jit(solution)/shard_map/pallas_call | solution.py:222
  2.3 8.8 %collective-permute-start = (f32[8,32,256]{2,1,0:T(8,128)}, f32[8,32,256]{2,1,0:T(8,128)S(1)}, u32[]{:S(2)}, u32[]{:S(2)}) collective-permute-start(f32[8,32,256]{2,1,0:T(8,128)} %get-tuple-element.15), channel_id=1, source_target_pairs={{0,1},{1,0},{2,3},{3,2},{4,5},{5,4},{6,7},{7,6},{8,9},{9,8},{10,11... | collective-permute-start | bytes 786440 | tf_op jit(solution)/shard_map/ppermute | solution.py:206
  11.0 1.4 collective-permute-done
  12.4 1.0 add.6
  13.4 14.8 %all_to_all.35 = f32[8,32,256]{2,1,0:T(8,128)S(1)} all-to-all(f32[8,32,256]{2,1,0:T(8,128)S(1)} %add.6), channel_id=1, replica_groups=mesh['rows'=32,'y'=8,'core'=2] {'y'}, dimensions={0} | all-to-all | bytes 524288 | tf_op jit(solution)/shard_map/all_to_all | solution.py:197
  28.1 0.0 copy-start
  28.2 16.6 %all_gather.3.sketch_ref = f32[512,256]{1,0:T(8,128)S(1)} all-gather(f32[32,256]{1,0:T(8,128)S(1)} %reduce_sum.36), channel_id=1, replica_groups=mesh['rows'=32,'y'=8,'core'=2] {'y','core'}, dimensions={0}, use_global_device_ids=true | all-gather | bytes 557056 | tf_op jit(solution)/shard_map/all_gather | solution.py:230
  44.7 0.0 copy-done
  44.7 1.1 shard_map.47
  45.8 28.3 %all_to_all.36 = f32[32,40,128]{2,1,0:T(8,128)S(1)} all-to-all(f32[32,40,128]{2,1,0:T(8,128)S(1)} %shard_map.47), channel_id=1, replica_groups=mesh['rows'=32,'y'=8,'core'=2] {'rows'}, dimensions={0} | all-to-all | bytes 1310720 | tf_op jit(solution)/shard_map/all_to_all | solution.py:197
  74.1 0.1 reduce_sum.37
  74.2 24.6 %all_to_all.37.both_ref = f32[32,40,128]{2,1,0:T(8,128)S(1)} all-to-all(f32[32,40,128]{2,1,0:T(8,128)S(1)} %broadcast_in_dim.6), channel_id=1, replica_groups=mesh['rows'=32,'y'=8,'core'=2] {'rows'}, dimensions={0} | all-to-all | bytes 1310720 | tf_op jit(solution)/shard_map/all_to_all | solution.py:197
  98.8 0.6 shard_map.48
  99.5 6.9 %collective-permute-start.1 = (f32[8,48,256]{2,1,0:T(8,128)S(1)}, f32[8,48,256]{2,1,0:T(8,128)S(1)}, u32[]{:S(2)}, u32[]{:S(2)}) collective-permute-start(f32[8,48,256]{2,1,0:T(8,128)S(1)} %get-tuple-element.17), channel_id=1, source_target_pairs={{0,1},{1,0},{2,3},{3,2},{4,5},{5,4},{6,7},{7,6},{8,9},{9,8},{10,11... | collective-permute-start | bytes 1179656 | tf_op jit(solution)/shard_map/ppermute | solution.py:206
  106.3 1.3 collective-permute-done.1.received_ref
  107.7 0.7 slice_add_fusion
  108.4 3.4 %all-to-all-start.3 = ((f32[8,32,256]{2,1,0:T(8,128)}), f32[8,32,256]{2,1,0:T(8,128)S(1)}, u32[]{:S(2)}, u32[]{:S(2)}) async-start(f32[8,32,256]{2,1,0:T(8,128)} %slice_add_fusion), calls=%async_computation.3 | async-start | bytes 524288 | tf_op jit(solution)/shard_map/all_to_all | solution.py:197
  111.8 6.1 %shard_map.49.inverse_ref = f32[256,256]{1,0:T(8,128)S(1)} custom-call(s32[1]{0:T(128)} %bitcast.core_ref, f32[256,128]{1,0:T(8,128)S(1)} %get-tuple-element.18.own_ref, f32[8,48,256]{2,1,0:T(8,128)S(1)} %collective-permute-done.1.received_ref), custom_call_target="tpu_custom_call" | custom-call | flops 10000000000 | bytes 1000000 | tf_op jit(solution)/shard_map/pallas_call | solution.py:250
  118.0 4.9 %all-to-all-done.3.parts_ref = f32[8,32,256]{2,1,0:T(8,128)S(1)} async-done(((f32[8,32,256]{2,1,0:T(8,128)}), f32[8,32,256]{2,1,0:T(8,128)S(1)}, u32[]{:S(2)}, u32[]{:S(2)}) %all-to-all-start.3) | async-done | bytes 262176 | tf_op jit(solution)/shard_map/all_to_all | solution.py:197
  122.9 1.1 shard_map.50
  124.0 13.9 %all_to_all.38 = f32[32,8,256]{2,1,0:T(8,128)S(1)} all-to-all(f32[32,8,256]{2,1,0:T(8,128)S(1)} %get-tuple-element.20), channel_id=1, replica_groups=mesh['rows'=32,'y'=8,'core'=2] {'rows'}, dimensions={0} | all-to-all | bytes 524288 | tf_op jit(solution)/shard_map/all_to_all | solution.py:197
  137.9 15.3 %all_to_all.39 = f32[16,8,256]{2,1,0:T(8,128)S(1)} all-to-all(f32[16,8,256]{2,1,0:T(8,128)S(1)} %broadcast_in_dim.7), channel_id=1, replica_groups=mesh['rows'=32,'y'=8,'core'=2] {'y','core'}, dimensions={0} | all-to-all | bytes 262144 | tf_op jit(solution)/shard_map/all_to_all | solution.py:197
  153.2 14.7 %all_to_all.40.refs_1_ = f32[32,8,256]{2,1,0:T(8,128)S(1)} all-to-all(f32[32,8,256]{2,1,0:T(8,128)S(1)} %broadcast_in_dim.8), channel_id=1, replica_groups=mesh['rows'=32,'y'=8,'core'=2] {'rows'}, dimensions={0} | all-to-all | bytes 524288 | tf_op jit(solution)/shard_map/all_to_all | solution.py:197
  168.0 6.8 %shard_map.51 = f32[32,256]{1,0:T(8,128)} custom-call(f32[32,256]{1,0:T(8,128)S(1)} %get-tuple-element.19.refs_0_, f32[32,8,256]{2,1,0:T(8,128)S(1)} %all_to_all.40.refs_1_), custom_call_target="tpu_custom_call" | custom-call | tf_op jit(solution)/shard_map/pallas_call | solution.py:268
  (6 shorter events, 0.2 us)
Async XLA Ops:
  2.3 10.1 %collective-permute-start = (f32[8,32,256]{2,1,0:T(8,128)}, f32[8,32,256]{2,1,0:T(8,128)S(1)}, u32[]{:S(2)}, u32[]{:S(2)}) collective-permute-start(f32[8,32,256]{2,1,0:T(8,128)} %get-tuple-element.15), channel_id=1, source_target_pairs={{0,1},{1,0},{2,3},{3,2},{4,5},{5,4},{6,7},{7,6},{8,9},{9,8},{10,11... | collective-permute-start | bytes 786440 | tf_op jit(solution)/shard_map/ppermute | solution.py:206
  28.1 16.6 %copy-start = (bf16[512,512]{1,0:T(8,128)(2,1)S(1)}, bf16[512,512]{1,0:T(8,128)(2,1)}, u32[]{:S(2)}) copy-start(bf16[512,512]{1,0:T(8,128)(2,1)} %get-tuple-element.13.tile_ref) | copy-start | bytes 1572868
  99.5 8.2 %collective-permute-start.1 = (f32[8,48,256]{2,1,0:T(8,128)S(1)}, f32[8,48,256]{2,1,0:T(8,128)S(1)}, u32[]{:S(2)}, u32[]{:S(2)}) collective-permute-start(f32[8,48,256]{2,1,0:T(8,128)S(1)} %get-tuple-element.17), channel_id=1, source_target_pairs={{0,1},{1,0},{2,3},{3,2},{4,5},{5,4},{6,7},{7,6},{8,9},{9,8},{10,11... | collective-permute-start | bytes 1179656 | tf_op jit(solution)/shard_map/ppermute | solution.py:206
  108.4 14.5 %all-to-all-start.3 = ((f32[8,32,256]{2,1,0:T(8,128)}), f32[8,32,256]{2,1,0:T(8,128)S(1)}, u32[]{:S(2)}, u32[]{:S(2)}) async-start(f32[8,32,256]{2,1,0:T(8,128)} %slice_add_fusion), calls=%async_computation.3 | async-start | bytes 524288 | tf_op jit(solution)/shard_map/all_to_all | solution.py:197

commit v6 on v5

--- a/solution.py
+++ b/solution.py
@@ -89,35 +89,37 @@
     return jnp.concatenate(done, axis=0)
 
 
-def factor(gram):
-    n = gram.shape[0]
-    half = n // 2
+def factor(first, lower, second):
+    n = first.shape[0]
     r = lax.broadcasted_iota(jnp.int32, (n, n), 0)
     c = lax.broadcasted_iota(jnp.int32, (n, n), 1)
-    diag = jnp.where(r == c, gram, 0.0)
-    across = lax.rsqrt(jnp.sum(diag, axis=0, keepdims=True))
-    down = lax.rsqrt(jnp.sum(diag, axis=1, keepdims=True))
-    unit = jnp.where(r == c, 1.0, gram * across * down)
-    first = block_inverse(unit[:half, :half])
-    lower = dot(unit[half:, :half], first, HIGHEST, (1, 1))
-    second = block_inverse(unit[half:, half:] - dot(lower, lower, HIGHEST, (1, 1)))
-    return across, first, lower, second
+    scales = []
+    for block in (first, second):
+        diag = jnp.where(r == c, block, 0.0)
+        scales.append([lax.rsqrt(jnp.sum(diag, axis=i, keepdims=True)) for i in (0, 1)])
+    (across1, down1), (across2, down2) = scales
+    inv1 = block_inverse(jnp.where(r == c, 1.0, first * across1 * down1))
+    lower = dot(lower * across1 * down2, inv1, HIGHEST, (1, 1))
+    second = jnp.where(r == c, 1.0, second * across2 * down2)
+    inv2 = block_inverse(second - dot(lower, lower, HIGHEST, (1, 1)))
+    return across1, across2, inv1, lower, inv2
 
 
 def inverse_factor(gram):
-    across, first, lower, second = factor(gram)
-    corner = -dot(second, dot(lower, first, HIGHEST), HIGHEST)
-    top = jnp.concatenate([first, jnp.zeros_like(first)], axis=1)
-    return jnp.concatenate([top, jnp.concatenate([corner, second], axis=1)], axis=0) * across
-
-
-def whiten(x, gram):
-    across, first, lower, second = factor(gram)
-    half = first.shape[0]
-    x = x * across
-    left = dot(x[:, :half], first, HIGHEST, (1, 1))
-    right = dot(x[:, half:] - dot(left, lower, HIGHEST, (1, 1)), second, HIGHEST, (1, 1))
+    half = gram.shape[0] // 2
+    across1, across2, inv1, lower, inv2 = factor(gram[:half, :half], gram[half:, :half], gram[half:, half:])
+    corner = -dot(inv2, dot(lower, inv1, HIGHEST), HIGHEST)
+    left = jnp.concatenate([inv1, corner], axis=0) * across1
+    right = jnp.concatenate([jnp.zeros_like(inv2), inv2], axis=0) * across2
     return jnp.concatenate([left, right], axis=1)
+
+
+def whiten(x, *blocks):
+    across1, across2, inv1, lower, inv2 = factor(*blocks)
+    half = inv1.shape[0]
+    left = dot(x[:, :half] * across1, inv1, HIGHEST, (1, 1))
+    right = x[:, half:] * across2 - dot(left, lower, HIGHEST, (1, 1))
+    return jnp.concatenate([left, dot(right, inv2, HIGHEST, (1, 1))], axis=1)
 
 
 def pick(core_ref, first, second):
@@ -182,12 +184,17 @@
 def gram_kernel(parts_ref, inverse_ref, share_ref, gram_ref):
     share = dot(jnp.sum(parts_ref[...], axis=0), inverse_ref[...], HIGHEST, (1, 1))
     share_ref[...] = share
-    gram_ref[...] = dot(share, share, HIGHEST, (0, 0)).reshape(gram_ref.shape)
+    gram = dot(share, share, HIGHEST, (0, 0))
+    half = gram.shape[0] // 2
+    gram_ref[: 2 * half, :] = gram[:, :half]
+    gram_ref[2 * half :, :] = gram[half:, half:]
 
 
 def final_kernel(scale, share_ref, gram_ref, out_ref):
-    rank = out_ref.shape[1]
-    out_ref[...] = whiten(share_ref[...], gram_ref[...].reshape(rank, rank)) * scale
+    gram = gram_ref[...]
+    half = gram.shape[1]
+    first, lower, second = gram[:half], gram[half : 2 * half], gram[2 * half :]
+    out_ref[...] = whiten(share_ref[...], first, lower, second) * scale
 
 
 FEAT = ("y", "core")
@@ -260,9 +267,10 @@
         gram_kernel,
         in_specs=[VMEM] * 2,
         out_specs=[VMEM] * 2,
-        out_shape=[f32(share, rank), f32(n_rows, rank // n_rows, rank)],
+        out_shape=[f32(share, rank), f32(3 * half, half)],
         compiler_params=PARAMS,
     )(parts, inverse)
+    gram = gram.reshape(n_rows, 3 * half // (4 * n_rows), 4, half)
     gram = jnp.sum(to_each(gram, "rows"), axis=0)
     gram = jnp.sum(from_each(gram, FEAT), axis=0)
     return pl.pallas_call(
@@ -271,7 +279,7 @@
         out_specs=VMEM,
         out_shape=f32(share, rank),
         compiler_params=PARAMS,
-    )(resketch, from_each(gram, "rows"))
+    )(resketch, from_each(gram, "rows").reshape(3 * half, half))
 
 
 def solution(mesh):

time: 176 us -> 173 us (0.983)
  blocking collectives: 128 us -> 125 us
    all_to_all x6, blocking collectives: 112 us -> 109 us  [to_each(): return lax.all_to_all(x, axis, 0, 0, tiled=True)]
where the time goes in v6:
time: 173 us; the launch traced here: 172 us
  blocking collectives  125 us (72%)
  starting transfers between devices  19 us (11%)
  Pallas kernels  18 us (10%)
  waiting for transfers between devices  7.58 us (4%)
  other arithmetic  1.88 us (1%)
    all_to_all x6, blocking collectives, to_each(): return lax.all_to_all(x, axis, 0, 0, tiled=True)  109 us
    all_gather x1, blocking collectives, per_device(): sketch = lax.all_gather(sketch, FEAT, axis=0, tiled=True)  16.6 us
    ppermute x2, starting transfers between devices, swap_cores(): return lax.ppermute(x, 'core', [(0, 1), (1, 0)])  15.6 us
    pallas_call x1, Pallas kernels, per_device(): pl.pallas_call(lambda *refs: final_kernel(scale, *refs), in_specs=[VMEM]...  6.8 us
    pallas_call x1, Pallas kernels, per_device(): pl.pallas_call(factor_kernel, in_specs=[SMEM, VMEM, VMEM], out_specs=VMEM...  6.13 us
    all_to_all x1, waiting for transfers between devices, to_each(): return lax.all_to_all(x, axis, 0, 0, tiled=True)  4.9 us
  transfers between devices with their start and end apart: 3, of which 3 were waited for; matrix products, arithmetic and copies ran while one was open for 0% of the time, Pallas kernels for 4%

profile of v6, /device:TPU:1, one launch (start us, length us, event | category | flops | bytes accessed | tf_op | source)
XLA Modules:
  0.0 172.2 jit_solution(12180505542365463129)
XLA Ops:
  0.0 2.3 %shard_map.46 = (bf16[512,512]{1,0:T(8,128)(2,1)}, f32[8,32,256]{2,1,0:T(8,128)}, f32[8,32,256]{2,1,0:T(8,128)}) custom-call(s32[12]{0:T(128)} %bitcast.9, s32[12]{0:T(128)} %bitcast.10, s32[1]{0:T(128)} %bitcast.core_ref, bf16[12,128,128]{2,1,0:T(8,128)(2,1)} %bitcast.8, bf16[512,256]{1,0:T(8,128)(2,1)} %test_ref.1), custom_call_target="tpu_custom_call" | custom-call | tf_op jit(solution)/shard_map/pallas_call | solution.py:229
  2.3 8.8 %collective-permute-start = (f32[8,32,256]{2,1,0:T(8,128)}, f32[8,32,256]{2,1,0:T(8,128)S(1)}, u32[]{:S(2)}, u32[]{:S(2)}) collective-permute-start(f32[8,32,256]{2,1,0:T(8,128)} %get-tuple-element.15), channel_id=1, source_target_pairs={{0,1},{1,0},{2,3},{3,2},{4,5},{5,4},{6,7},{7,6},{8,9},{9,8},{10,11... | collective-permute-start | bytes 786440 | tf_op jit(solution)/shard_map/ppermute | solution.py:213
  11.0 1.4 collective-permute-done
  12.4 1.0 add.6
  13.4 14.8 %all_to_all.35 = f32[8,32,256]{2,1,0:T(8,128)S(1)} all-to-all(f32[8,32,256]{2,1,0:T(8,128)S(1)} %add.6), channel_id=1, replica_groups=mesh['rows'=32,'y'=8,'core'=2] {'y'}, dimensions={0} | all-to-all | bytes 524288 | tf_op jit(solution)/shard_map/all_to_all | solution.py:204
  28.1 0.0 copy-start
  28.2 16.6 %all_gather.3.sketch_ref = f32[512,256]{1,0:T(8,128)S(1)} all-gather(f32[32,256]{1,0:T(8,128)S(1)} %reduce_sum.36), channel_id=1, replica_groups=mesh['rows'=32,'y'=8,'core'=2] {'y','core'}, dimensions={0}, use_global_device_ids=true | all-gather | bytes 557056 | tf_op jit(solution)/shard_map/all_gather | solution.py:237
  44.7 0.0 copy-done
  44.7 1.1 shard_map.47
  45.8 28.3 %all_to_all.36 = f32[32,40,128]{2,1,0:T(8,128)S(1)} all-to-all(f32[32,40,128]{2,1,0:T(8,128)S(1)} %shard_map.47), channel_id=1, replica_groups=mesh['rows'=32,'y'=8,'core'=2] {'rows'}, dimensions={0} | all-to-all | bytes 1310720 | tf_op jit(solution)/shard_map/all_to_all | solution.py:204
  74.1 0.1 reduce_sum.37
  74.2 24.6 %all_to_all.37.both_ref = f32[32,40,128]{2,1,0:T(8,128)S(1)} all-to-all(f32[32,40,128]{2,1,0:T(8,128)S(1)} %broadcast_in_dim.6), channel_id=1, replica_groups=mesh['rows'=32,'y'=8,'core'=2] {'rows'}, dimensions={0} | all-to-all | bytes 1310720 | tf_op jit(solution)/shard_map/all_to_all | solution.py:204
  98.8 0.6 shard_map.48
  99.5 6.9 %collective-permute-start.1 = (f32[8,48,256]{2,1,0:T(8,128)S(1)}, f32[8,48,256]{2,1,0:T(8,128)S(1)}, u32[]{:S(2)}, u32[]{:S(2)}) collective-permute-start(f32[8,48,256]{2,1,0:T(8,128)S(1)} %get-tuple-element.17), channel_id=1, source_target_pairs={{0,1},{1,0},{2,3},{3,2},{4,5},{5,4},{6,7},{7,6},{8,9},{9,8},{10,11... | collective-permute-start | bytes 1179656 | tf_op jit(solution)/shard_map/ppermute | solution.py:213
  106.3 1.3 collective-permute-done.1.received_ref
  107.7 0.7 slice_add_fusion
  108.4 3.4 %all-to-all-start.3 = ((f32[8,32,256]{2,1,0:T(8,128)}), f32[8,32,256]{2,1,0:T(8,128)S(1)}, u32[]{:S(2)}, u32[]{:S(2)}) async-start(f32[8,32,256]{2,1,0:T(8,128)} %slice_add_fusion), calls=%async_computation.3 | async-start | bytes 524288 | tf_op jit(solution)/shard_map/all_to_all | solution.py:204
  111.8 6.1 %shard_map.49.inverse_ref = f32[256,256]{1,0:T(8,128)S(1)} custom-call(s32[1]{0:T(128)} %bitcast.core_ref, f32[256,128]{1,0:T(8,128)S(1)} %get-tuple-element.18.own_ref, f32[8,48,256]{2,1,0:T(8,128)S(1)} %collective-permute-done.1.received_ref), custom_call_target="tpu_custom_call" | custom-call | flops 10000000000 | bytes 1000000 | tf_op jit(solution)/shard_map/pallas_call | solution.py:257
  118.0 4.9 %all-to-all-done.3.parts_ref = f32[8,32,256]{2,1,0:T(8,128)S(1)} async-done(((f32[8,32,256]{2,1,0:T(8,128)}), f32[8,32,256]{2,1,0:T(8,128)S(1)}, u32[]{:S(2)}, u32[]{:S(2)}) %all-to-all-start.3) | async-done | bytes 262176 | tf_op jit(solution)/shard_map/all_to_all | solution.py:204
  122.9 1.1 shard_map.50
  124.0 13.6 %all_to_all.38 = f32[32,3,4,128]{3,2,1,0:T(4,128)S(1)} all-to-all(f32[32,3,4,128]{3,2,1,0:T(4,128)S(1)} %bitcast.7), channel_id=1, replica_groups=mesh['rows'=32,'y'=8,'core'=2] {'rows'}, dimensions={0} | all-to-all | bytes 393216 | tf_op jit(solution)/shard_map/all_to_all | solution.py:204
  137.6 0.1 reduce_sum.38
  137.7 14.3 %all_to_all.39 = f32[16,3,4,128]{3,2,1,0:T(4,128)S(1)} all-to-all(f32[16,3,4,128]{3,2,1,0:T(4,128)S(1)} %broadcast_in_dim.7), channel_id=1, replica_groups=mesh['rows'=32,'y'=8,'core'=2] {'y','core'}, dimensions={0} | all-to-all | bytes 196608 | tf_op jit(solution)/shard_map/all_to_all | solution.py:204
  152.0 13.4 %all_to_all.40 = f32[32,3,4,128]{3,2,1,0:T(4,128)S(1)} all-to-all(f32[32,3,4,128]{3,2,1,0:T(4,128)S(1)} %broadcast_in_dim.8), channel_id=1, replica_groups=mesh['rows'=32,'y'=8,'core'=2] {'rows'}, dimensions={0} | all-to-all | bytes 393216 | tf_op jit(solution)/shard_map/all_to_all | solution.py:204
  165.4 6.8 %shard_map.51 = f32[32,256]{1,0:T(8,128)} custom-call(f32[32,256]{1,0:T(8,128)S(1)} %get-tuple-element.19.refs_0_, f32[384,128]{1,0:T(8,128)S(1)} %bitcast.6), custom_call_target="tpu_custom_call" | custom-call | tf_op jit(solution)/shard_map/pallas_call | solution.py:276
  (5 shorter events, 0.1 us)
Async XLA Ops:
  2.3 10.1 %collective-permute-start = (f32[8,32,256]{2,1,0:T(8,128)}, f32[8,32,256]{2,1,0:T(8,128)S(1)}, u32[]{:S(2)}, u32[]{:S(2)}) collective-permute-start(f32[8,32,256]{2,1,0:T(8,128)} %get-tuple-element.15), channel_id=1, source_target_pairs={{0,1},{1,0},{2,3},{3,2},{4,5},{5,4},{6,7},{7,6},{8,9},{9,8},{10,11... | collective-permute-start | bytes 786440 | tf_op jit(solution)/shard_map/ppermute | solution.py:213
  28.1 16.6 %copy-start = (bf16[512,512]{1,0:T(8,128)(2,1)S(1)}, bf16[512,512]{1,0:T(8,128)(2,1)}, u32[]{:S(2)}) copy-start(bf16[512,512]{1,0:T(8,128)(2,1)} %get-tuple-element.13.tile_ref) | copy-start | bytes 1572868
  99.5 8.2 %collective-permute-start.1 = (f32[8,48,256]{2,1,0:T(8,128)S(1)}, f32[8,48,256]{2,1,0:T(8,128)S(1)}, u32[]{:S(2)}, u32[]{:S(2)}) collective-permute-start(f32[8,48,256]{2,1,0:T(8,128)S(1)} %get-tuple-element.17), channel_id=1, source_target_pairs={{0,1},{1,0},{2,3},{3,2},{4,5},{5,4},{6,7},{7,6},{8,9},{9,8},{10,11... | collective-permute-start | bytes 1179656 | tf_op jit(solution)/shard_map/ppermute | solution.py:213
  108.4 14.5 %all-to-all-start.3 = ((f32[8,32,256]{2,1,0:T(8,128)}), f32[8,32,256]{2,1,0:T(8,128)S(1)}, u32[]{:S(2)}, u32[]{:S(2)}) async-start(f32[8,32,256]{2,1,0:T(8,128)} %slice_add_fusion), calls=%async_computation.3 | async-start | bytes 524288 | tf_op jit(solution)/shard_map/all_to_all | solution.py:204

commit v7 on v6

--- a/solution.py
+++ b/solution.py
@@ -122,6 +122,10 @@
     return jnp.concatenate([left, dot(right, inv2, HIGHEST, (1, 1))], axis=1)
 
 
+def square(n):
+    return lax.broadcasted_iota(jnp.int32, (n, n), 0), lax.broadcasted_iota(jnp.int32, (n, n), 1)
+
+
 def pick(core_ref, first, second):
     return jnp.where(core_ref[0] == 0, first, second)
 
@@ -186,14 +190,23 @@
     share_ref[...] = share
     gram = dot(share, share, HIGHEST, (0, 0))
     half = gram.shape[0] // 2
-    gram_ref[: 2 * half, :] = gram[:, :half]
-    gram_ref[2 * half :, :] = gram[half:, half:]
+    r, c = square(half)
+    last = gram[half:, half:]
+    gram_ref[:half, :] = jnp.where(r >= c, gram[:half, :half], last)
+    gram_ref[half : 2 * half, :] = gram[half:, :half]
+    diag = jnp.sum(jnp.where(r == c, last, 0.0), axis=0, keepdims=True)
+    spare = gram_ref.shape[0] - 2 * half
+    gram_ref[2 * half :, :] = jnp.broadcast_to(diag, (spare, half))
 
 
 def final_kernel(scale, share_ref, gram_ref, out_ref):
     gram = gram_ref[...]
     half = gram.shape[1]
-    first, lower, second = gram[:half], gram[half : 2 * half], gram[2 * half :]
+    r, c = square(half)
+    packed, lower = gram[:half], gram[half : 2 * half]
+    mirror = packed.T
+    first = jnp.where(r >= c, packed, mirror)
+    second = jnp.where(r == c, gram[2 * half : 2 * half + 1], jnp.where(r < c, packed, mirror))
     out_ref[...] = whiten(share_ref[...], first, lower, second) * scale
 
 
@@ -267,10 +280,10 @@
         gram_kernel,
         in_specs=[VMEM] * 2,
         out_specs=[VMEM] * 2,
-        out_shape=[f32(share, rank), f32(3 * half, half)],
+        out_shape=[f32(share, rank), f32(rank + n_rows, half)],
         compiler_params=PARAMS,
     )(parts, inverse)
-    gram = gram.reshape(n_rows, 3 * half // (4 * n_rows), 4, half)
+    gram = gram.reshape(n_rows, rank // n_rows + 1, 1, half)
     gram = jnp.sum(to_each(gram, "rows"), axis=0)
     gram = jnp.sum(from_each(gram, FEAT), axis=0)
     return pl.pallas_call(
@@ -279,7 +292,7 @@
         out_specs=VMEM,
         out_shape=f32(share, rank),
         compiler_params=PARAMS,
-    )(resketch, from_each(gram, "rows").reshape(3 * half, half))
+    )(resketch, from_each(gram, "rows").reshape(rank + n_rows, half))
 
 
 def solution(mesh):

time: 173 us -> 171 us (0.988)
  no operation moved by 1% of the time
where the time goes in v7:
time: 171 us
  blocking collectives  124 us (73%)
  starting transfers between devices  19 us (11%)
  Pallas kernels  18.1 us (11%)
  waiting for transfers between devices  7.58 us (4%)
  other arithmetic  1.95 us (1%)
    all_to_all x6, blocking collectives, to_each(): return lax.all_to_all(x, axis, 0, 0, tiled=True)  107 us
    all_gather x1, blocking collectives, per_device(): sketch = lax.all_gather(sketch, FEAT, axis=0, tiled=True)  16.6 us
    ppermute x2, starting transfers between devices, swap_cores(): return lax.ppermute(x, 'core', [(0, 1), (1, 0)])  15.6 us
    pallas_call x1, Pallas kernels, per_device(): pl.pallas_call(lambda *refs: final_kernel(scale, *refs), in_specs=[VMEM]...  6.88 us
    pallas_call x1, Pallas kernels, per_device(): pl.pallas_call(factor_kernel, in_specs=[SMEM, VMEM, VMEM], out_specs=VMEM...  6.13 us
    all_to_all x1, waiting for transfers between devices, to_each(): return lax.all_to_all(x, axis, 0, 0, tiled=True)  4.9 us
  transfers between devices with their start and end apart: 3, of which 3 were waited for; matrix products, arithmetic and copies ran while one was open for 0% of the time, Pallas kernels for 4%

profile of v7, /device:TPU:1, one launch (start us, length us, event | category | flops | bytes accessed | tf_op | source)
XLA Modules:
  0.0 170.8 jit_solution(8547768115379166466)
XLA Ops:
  0.0 2.3 %shard_map.46 = (bf16[512,512]{1,0:T(8,128)(2,1)}, f32[8,32,256]{2,1,0:T(8,128)}, f32[8,32,256]{2,1,0:T(8,128)}) custom-call(s32[12]{0:T(128)} %bitcast.9, s32[12]{0:T(128)} %bitcast.10, s32[1]{0:T(128)} %bitcast.core_ref, bf16[12,128,128]{2,1,0:T(8,128)(2,1)} %bitcast.8, bf16[512,256]{1,0:T(8,128)(2,1)} %test_ref.1), custom_call_target="tpu_custom_call" | custom-call | tf_op jit(solution)/shard_map/pallas_call | solution.py:242
  2.3 8.8 %collective-permute-start = (f32[8,32,256]{2,1,0:T(8,128)}, f32[8,32,256]{2,1,0:T(8,128)S(1)}, u32[]{:S(2)}, u32[]{:S(2)}) collective-permute-start(f32[8,32,256]{2,1,0:T(8,128)} %get-tuple-element.15), channel_id=1, source_target_pairs={{0,1},{1,0},{2,3},{3,2},{4,5},{5,4},{6,7},{7,6},{8,9},{9,8},{10,11... | collective-permute-start | bytes 786440 | tf_op jit(solution)/shard_map/ppermute | solution.py:226
  11.0 1.4 collective-permute-done
  12.4 1.0 add.6
  13.4 14.8 %all_to_all.35 = f32[8,32,256]{2,1,0:T(8,128)S(1)} all-to-all(f32[8,32,256]{2,1,0:T(8,128)S(1)} %add.6), channel_id=1, replica_groups=mesh['rows'=32,'y'=8,'core'=2] {'y'}, dimensions={0} | all-to-all | bytes 524288 | tf_op jit(solution)/shard_map/all_to_all | solution.py:217
  28.1 0.0 copy-start
  28.2 16.6 %all_gather.3.sketch_ref = f32[512,256]{1,0:T(8,128)S(1)} all-gather(f32[32,256]{1,0:T(8,128)S(1)} %reduce_sum.36), channel_id=1, replica_groups=mesh['rows'=32,'y'=8,'core'=2] {'y','core'}, dimensions={0}, use_global_device_ids=true | all-gather | bytes 557056 | tf_op jit(solution)/shard_map/all_gather | solution.py:250
  44.7 0.0 copy-done
  44.7 1.1 shard_map.47
  45.8 28.3 %all_to_all.36 = f32[32,40,128]{2,1,0:T(8,128)S(1)} all-to-all(f32[32,40,128]{2,1,0:T(8,128)S(1)} %shard_map.47), channel_id=1, replica_groups=mesh['rows'=32,'y'=8,'core'=2] {'rows'}, dimensions={0} | all-to-all | bytes 1310720 | tf_op jit(solution)/shard_map/all_to_all | solution.py:217
  74.1 0.1 reduce_sum.37
  74.2 24.6 %all_to_all.37.both_ref = f32[32,40,128]{2,1,0:T(8,128)S(1)} all-to-all(f32[32,40,128]{2,1,0:T(8,128)S(1)} %broadcast_in_dim.6), channel_id=1, replica_groups=mesh['rows'=32,'y'=8,'core'=2] {'rows'}, dimensions={0} | all-to-all | bytes 1310720 | tf_op jit(solution)/shard_map/all_to_all | solution.py:217
  98.8 0.6 shard_map.48
  99.5 6.9 %collective-permute-start.1 = (f32[8,48,256]{2,1,0:T(8,128)S(1)}, f32[8,48,256]{2,1,0:T(8,128)S(1)}, u32[]{:S(2)}, u32[]{:S(2)}) collective-permute-start(f32[8,48,256]{2,1,0:T(8,128)S(1)} %get-tuple-element.17), channel_id=1, source_target_pairs={{0,1},{1,0},{2,3},{3,2},{4,5},{5,4},{6,7},{7,6},{8,9},{9,8},{10,11... | collective-permute-start | bytes 1179656 | tf_op jit(solution)/shard_map/ppermute | solution.py:226
  106.3 1.3 collective-permute-done.1.received_ref
  107.7 0.7 slice_add_fusion
  108.4 3.4 %all-to-all-start.3 = ((f32[8,32,256]{2,1,0:T(8,128)}), f32[8,32,256]{2,1,0:T(8,128)S(1)}, u32[]{:S(2)}, u32[]{:S(2)}) async-start(f32[8,32,256]{2,1,0:T(8,128)} %slice_add_fusion), calls=%async_computation.3 | async-start | bytes 524288 | tf_op jit(solution)/shard_map/all_to_all | solution.py:217
  111.8 6.1 %shard_map.49.inverse_ref = f32[256,256]{1,0:T(8,128)S(1)} custom-call(s32[1]{0:T(128)} %bitcast.core_ref, f32[256,128]{1,0:T(8,128)S(1)} %get-tuple-element.18.own_ref, f32[8,48,256]{2,1,0:T(8,128)S(1)} %collective-permute-done.1.received_ref), custom_call_target="tpu_custom_call" | custom-call | flops 10000000000 | bytes 1000000 | tf_op jit(solution)/shard_map/pallas_call | solution.py:270
  118.0 4.9 %all-to-all-done.3.parts_ref = f32[8,32,256]{2,1,0:T(8,128)S(1)} async-done(((f32[8,32,256]{2,1,0:T(8,128)}), f32[8,32,256]{2,1,0:T(8,128)S(1)}, u32[]{:S(2)}, u32[]{:S(2)}) %all-to-all-start.3) | async-done | bytes 262176 | tf_op jit(solution)/shard_map/all_to_all | solution.py:217
  122.9 1.1 shard_map.50
  124.0 13.4 %all_to_all.38 = f32[32,9,1,128]{3,2,1,0:T(1,128)S(1)} all-to-all(f32[32,9,1,128]{3,2,1,0:T(1,128)S(1)} %bitcast.7), channel_id=1, replica_groups=mesh['rows'=32,'y'=8,'core'=2] {'rows'}, dimensions={0} | all-to-all | bytes 294912 | tf_op jit(solution)/shard_map/all_to_all | solution.py:217
  137.4 0.1 reduce_sum.38
  137.6 13.7 %all_to_all.39 = f32[16,9,1,128]{3,2,1,0:T(1,128)S(1)} all-to-all(f32[16,9,1,128]{3,2,1,0:T(1,128)S(1)} %broadcast_in_dim.7), channel_id=1, replica_groups=mesh['rows'=32,'y'=8,'core'=2] {'y','core'}, dimensions={0} | all-to-all | bytes 147456 | tf_op jit(solution)/shard_map/all_to_all | solution.py:217
  151.2 0.1 reduce_sum.39
  151.3 0.1 broadcast_in_dim.8
  151.4 12.5 %all_to_all.40 = f32[32,9,1,128]{3,2,1,0:T(1,128)S(1)} all-to-all(f32[32,9,1,128]{3,2,1,0:T(1,128)S(1)} %broadcast_in_dim.8), channel_id=1, replica_groups=mesh['rows'=32,'y'=8,'core'=2] {'rows'}, dimensions={0} | all-to-all | bytes 294912 | tf_op jit(solution)/shard_map/all_to_all | solution.py:217
  163.9 6.9 %shard_map.51 = f32[32,256]{1,0:T(8,128)} custom-call(f32[32,256]{1,0:T(8,128)S(1)} %get-tuple-element.19.refs_0_, f32[288,128]{1,0:T(8,128)S(1)} %bitcast.6), custom_call_target="tpu_custom_call" | custom-call | tf_op jit(solution)/shard_map/pallas_call | solution.py:289
  (3 shorter events, 0.1 us)
Async XLA Ops:
  2.3 10.1 %collective-permute-start = (f32[8,32,256]{2,1,0:T(8,128)}, f32[8,32,256]{2,1,0:T(8,128)S(1)}, u32[]{:S(2)}, u32[]{:S(2)}) collective-permute-start(f32[8,32,256]{2,1,0:T(8,128)} %get-tuple-element.15), channel_id=1, source_target_pairs={{0,1},{1,0},{2,3},{3,2},{4,5},{5,4},{6,7},{7,6},{8,9},{9,8},{10,11... | collective-permute-start | bytes 786440 | tf_op jit(solution)/shard_map/ppermute | solution.py:226
  28.1 16.6 %copy-start = (bf16[512,512]{1,0:T(8,128)(2,1)S(1)}, bf16[512,512]{1,0:T(8,128)(2,1)}, u32[]{:S(2)}) copy-start(bf16[512,512]{1,0:T(8,128)(2,1)} %get-tuple-element.13.tile_ref) | copy-start | bytes 1572868
  99.5 8.2 %collective-permute-start.1 = (f32[8,48,256]{2,1,0:T(8,128)S(1)}, f32[8,48,256]{2,1,0:T(8,128)S(1)}, u32[]{:S(2)}, u32[]{:S(2)}) collective-permute-start(f32[8,48,256]{2,1,0:T(8,128)S(1)} %get-tuple-element.17), channel_id=1, source_target_pairs={{0,1},{1,0},{2,3},{3,2},{4,5},{5,4},{6,7},{7,6},{8,9},{9,8},{10,11... | collective-permute-start | bytes 1179656 | tf_op jit(solution)/shard_map/ppermute | solution.py:226
  108.4 14.5 %all-to-all-start.3 = ((f32[8,32,256]{2,1,0:T(8,128)}), f32[8,32,256]{2,1,0:T(8,128)S(1)}, u32[]{:S(2)}, u32[]{:S(2)}) async-start(f32[8,32,256]{2,1,0:T(8,128)} %slice_add_fusion), calls=%async_computation.3 | async-start | bytes 524288 | tf_op jit(solution)/shard_map/all_to_all | solution.py:217
